TPU v7x, 1024 devices: a whole 4x8x16 slice. The times are simulated.
1024 devices in a mesh: dp: 32 (over x, y), replica: 32 (over z, core).
Axes of the slice: x: 4, y: 8, z: 16, core: 2. Of those that a mesh axis runs over, the one named last changes fastest.
Arguments:
- grads: bfloat16 [32, 64, 512, 512], P('dp', None, 'replica'), may hold values from -2.5 to 2.5
- assignment: int32 [64, 1], replicated, may hold values from 0 to 31; in each aligned block of 64 rows (0 to 63, 64 to 127, ...) at most 4 rows name the same one
- left_stats: float32 [128, 512, 512], P('dp', 'replica'), may hold values from -12 to 12
- right_stats: float32 [128, 512, 512], P('dp', 'replica'), may hold values from -12 to 12
- second_moment: float32 [128, 512, 512], P('dp', 'replica'), may hold values from 0.1 to 10
- left_root: bfloat16 [128, 512, 512], P('dp', 'replica'), may hold values from -1 to 4, as said below
- right_root: bfloat16 [128, 512, 512], P('dp', 'replica'), may hold values from -1 to 4, as said below
Outputs:
- left_new: float32 [128, 512, 512], P('dp', 'replica')
- right_new: float32 [128, 512, 512], P('dp', 'replica')
- moment_new: float32 [128, 512, 512], P('dp', 'replica')
- direction: bfloat16 [128, 512, 512], P('dp', 'replica')
Inputs may be any that keep to these rules, and one draw needn't show every extreme that they name: `assignment`: no owner is named by more than 4 blocks, a bound that some block reaches. `left_root`: each slot's matrix is symmetric. `right_root`: each slot's matrix is symmetric.
All inputs are finite; a program needn't handle non-finite values.
Results may differ from a plain program's by a relative error of at most 0.025.
Values may be sent and summed in bfloat16 or wider, within the bound.
A program may use at most 32 MiB of HBM per device.

v0:
```python
import jax
import jax.numpy as jnp
from jax import lax
from jax.sharding import PartitionSpec as P


def owner_table(owner, owners):
    onehot = (owner[:, None] == jnp.arange(owners, dtype=jnp.int32)[None, :]).astype(jnp.int32)
    before = jnp.cumsum(onehot, axis=0) - onehot
    rank = jnp.sum(before * onehot, axis=1)
    counts = jnp.sum(onehot, axis=0)
    starts = jnp.cumsum(counts) - counts
    return (rank, counts, starts)


def on_device(grads, assignment, left_stats, right_stats, second_moment, left_root, right_root):
    most = left_stats.shape[0]
    rows = left_stats.shape[1]
    width = left_stats.shape[2]
    blocks = grads.shape[1]
    owners = lax.axis_size("dp")
    owner = assignment[:, 0]
    rank, counts, starts = owner_table(owner, owners)
    slot = owner * most + rank
    local = grads[0]
    numbers = jnp.arange(blocks, dtype=jnp.int32)
    wanted = jnp.arange(lax.axis_size("dp") * most, dtype=jnp.int32)
    match = (slot[:, None] == wanted[None, :]).astype(jnp.int32)
    source = jnp.sum(match * numbers[:, None], axis=0)
    filled = jnp.sum(match, axis=0).astype(jnp.float32)
    picked = jnp.take(local, source, axis=0).astype(jnp.float32)
    summed = lax.psum_scatter(
        (picked * filled[:, None, None]).astype(jnp.bfloat16), "dp", scatter_dimension=0, tiled=True
    )
    mine = lax.axis_index("replica") * rows
    piece = lax.all_gather(summed, "replica", axis=1, tiled=True)
    cross = jnp.einsum("kib,kjb->kij", summed, piece, preferred_element_type=jnp.float32)
    left_gram = cross
    own_cols = lax.dynamic_slice_in_dim(piece, mine, rows, 2)
    right_gram = jnp.einsum("kjc,kjb->kcb", own_cols, piece, preferred_element_type=jnp.float32)
    product = jnp.einsum("kij,kjb->kib", left_root, piece, preferred_element_type=jnp.float32)
    left_gram, right_gram, product = (left_gram, right_gram, product)
    left_new = 0.9 * left_stats + 0.1 * left_gram
    right_new = 0.9 * right_stats + 0.1 * right_gram
    wide = summed.astype(jnp.float32)
    moment_new = 0.95 * second_moment + 0.05 * wide * wide
    adam = wide / (jnp.sqrt(moment_new) + 1e-08)
    adam_squares = jnp.sum(adam * adam, axis=(1, 2))
    left_product = product.astype(jnp.bfloat16)
    part_rows = jnp.einsum(
        "kpa,kca->kpc",
        lax.all_gather(left_product, "replica", axis=1, tiled=True),
        right_root,
        preferred_element_type=jnp.float32,
    )
    shaped_squares = jnp.sum(part_rows * part_rows, axis=(1, 2))
    adam_total, shaped_total = lax.psum((adam_squares, shaped_squares), "replica")
    entries = float(width * width)
    ratio = jnp.sqrt(adam_total / entries) / jnp.sqrt(shaped_total / entries + 1e-06)
    direction = (part_rows * ratio[:, None, None]).astype(jnp.bfloat16)
    direction = lax.all_to_all(direction, "replica", split_axis=1, concat_axis=2, tiled=True)
    return (left_new, right_new, moment_new, direction)


def solution(mesh):
    in_specs = (
        P("dp", None, "replica", None),
        P(),
        P("dp", "replica", None),
        P("dp", "replica", None),
        P("dp", "replica", None),
        P("dp", "replica", None),
        P("dp", "replica", None),
    )
    out_specs = (
        P("dp", "replica", None),
        P("dp", "replica", None),
        P("dp", "replica", None),
        P("dp", "replica", None),
    )
    return jax.shard_map(
        on_device, mesh=mesh, in_specs=in_specs, out_specs=out_specs, check_vma=False
    )
```

profile of v0, /device:TPU:1, one launch (start us, length us, event | category | flops | bytes accessed | tf_op | source)
XLA Modules:
  0.0 490.3 jit_solution(18118580063705273624)
XLA Ops:
  7.2 0.0 copy-start
  7.2 0.0 reduce-scatter.2.cloned.1.call-start
  7.2 0.8 fusion.7
  8.0 0.1 reduce_window_sum.11
  8.1 0.8 select_reduce_fusion.1
  9.0 0.7 fusion.9
  9.6 0.1 select_reduce_fusion
  9.8 0.7 gather_fusion
  10.5 1.9 multiply_convert_fusion
  12.4 0.0 reduce-scatter.2.cloned.1.call-update
  12.4 0.0 all-gather.3.cloned.1.call-start
  12.5 236.5 %reduce-scatter.2.cloned.1.call-done = bf16[4,16,512]{2,1,0:T(8,128)(2,1)} async-done(((bf16[128,16,512]{2,1,0:T(8,128)(2,1)}), bf16[4,16,512]{2,1,0:T(8,128)(2,1)}) %reduce-scatter.2.cloned.1.call-update) | async-done | bytes 65552 | tf_op jit(solution)/shard_map/reduce_scatter | solution.py:32
  249.0 0.0 all-gather.3.cloned.1.call-update
  249.0 0.0 all-gather.5.cloned.1.call-start
  249.0 83.2 %all-gather.3.cloned.1.call-done = bf16[4,512,512]{2,1,0:T(8,128)(2,1)} async-done(((bf16[4,16,512]{2,1,0:T(8,128)(2,1)}), bf16[4,512,512]{2,1,0:T(8,128)(2,1)}) %all-gather.3.cloned.1.call-update) | async-done | bytes 2097168 | tf_op jit(solution)/shard_map/all_gather | solution.py:36
  332.2 2.8 fusion.2
  335.0 0.0 all-gather.5.cloned.1.call-update
  335.0 0.7 fusion.6
  335.7 0.0 copy-done.1
  335.7 1.3 fusion.1
  337.1 70.7 %all-gather.5.cloned.1.call-done = bf16[4,512,512]{2,1,0:T(8,128)(2,1)} async-done(((bf16[4,16,512]{2,1,0:T(8,128)(2,1)}), bf16[4,512,512]{2,1,0:T(8,128)(2,1)}) %all-gather.5.cloned.1.call-update) | async-done | bytes 2097168 | tf_op jit(solution)/shard_map/all_gather | solution.py:52
  407.8 2.3 multiply_reduce_fusion
  410.1 45.4 %all-reduce = (f32[4]{0:T(128)S(1)}, f32[4]{0:T(128)S(1)}) all-reduce(f32[4]{0:T(128)S(1)} %get-tuple-element.10, f32[4]{0:T(128)S(1)} %get-tuple-element.8), channel_id=1, replica_groups=mesh['dp'=32,'replica'=32] {'replica'}, use_global_device_ids=true, to_apply=%region_8.9 | all-reduce | flops 8 | bytes 64 | tf_op jit(solution)/shard_map/psum | solution.py:57
  455.6 0.1 multiply_convert_fusion.1
  455.6 1.1 copy.20
  456.7 2.2 reshape.39
  458.9 9.7 %all-to-all-start = ((bf16[32,2,512]{2,1,0:T(2,128)(2,1)}), bf16[32,2,512]{2,1,0:T(2,128)(2,1)S(1)}, u32[]{:S(2)}, u32[]{:S(2)}) async-start(bf16[32,2,512]{2,1,0:T(2,128)(2,1)} %reshape.39), calls=%async_computation.1 | async-start | bytes 131072 | tf_op jit(solution)/shard_map/all_to_all | solution.py:61
  468.6 1.3 fusion
  469.9 11.8 %all-to-all-done = bf16[32,2,512]{2,1,0:T(2,128)(2,1)S(1)} async-done(((bf16[32,2,512]{2,1,0:T(2,128)(2,1)}), bf16[32,2,512]{2,1,0:T(2,128)(2,1)S(1)}, u32[]{:S(2)}, u32[]{:S(2)}) %all-to-all-start) | async-done | bytes 65568 | tf_op jit(solution)/shard_map/all_to_all | solution.py:61
  481.7 0.4 reshape.40
  482.1 0.3 copy.27
  482.4 1.4 all_to_all.16
  (17 shorter events, 0.1 us)
Async XLA Ops:
  7.2 2.6 copy-start
  7.2 241.8 %reduce-scatter.2.cloned.1.call-start = ((), (), s32[]{:S(2)}) async-start(), calls=%async_computation.2 | async-start | bytes 2162688 | tf_op jit(solution)/shard_map/reduce_scatter | solution.py:32
  12.4 319.8 %copy-start.6 = (bf16[4,16,512]{2,1,0:T(8,128)(2,1)S(1)}, bf16[4,16,512]{2,1,0:T(8,128)(2,1)}, u32[]{:S(2)}) copy-start(bf16[4,16,512]{2,1,0:T(8,128)(2,1)} %param.12) | copy-start | bytes 196612
  12.4 322.6 %copy-start.3 = (f32[4,16,512]{2,1,0:T(8,128)S(1)}, f32[4,16,512]{2,1,0:T(8,128)}, u32[]{:S(2)}) copy-start(f32[4,16,512]{2,1,0:T(8,128)} %param.11) | copy-start | bytes 393220
  12.4 323.3 %copy-start.4 = (f32[4,16,512]{2,1,0:T(8,128)S(1)}, f32[4,16,512]{2,1,0:T(8,128)}, u32[]{:S(2)}) copy-start(f32[4,16,512]{2,1,0:T(8,128)} %param.9) | copy-start | bytes 393220
  12.4 319.8 %all-gather.3.cloned.1.call-start = ((), (), s32[]{:S(2)}) async-start(), calls=%async_computation.3 | async-start | bytes 2162688 | tf_op jit(solution)/shard_map/all_gather | solution.py:36
  249.0 86.0 %copy-start.2 = (bf16[4,16,512]{2,1,0:T(8,128)(2,1)S(1)}, bf16[4,16,512]{2,1,0:T(8,128)(2,1)}, u32[]{:S(2)}) copy-start(bf16[4,16,512]{2,1,0:T(8,128)(2,1)} %reduce-scatter.2.cloned.1.call-done) | copy-start | bytes 196612
  249.0 158.8 %all-gather.5.cloned.1.call-start = ((), (), s32[]{:S(2)}) async-start(), calls=%async_computation.4 | async-start | bytes 2162688 | tf_op jit(solution)/shard_map/all_gather | solution.py:52
  332.2 3.5 copy-start.1
  337.1 131.6 %copy-start.5 = (f32[4,16,512]{2,1,0:T(8,128)S(1)}, f32[4,16,512]{2,1,0:T(8,128)}, u32[]{:S(2)}) copy-start(f32[4,16,512]{2,1,0:T(8,128)} %param.10) | copy-start | bytes 393220
  458.9 22.8 %all-to-all-start = ((bf16[32,2,512]{2,1,0:T(2,128)(2,1)}), bf16[32,2,512]{2,1,0:T(2,128)(2,1)S(1)}, u32[]{:S(2)}, u32[]{:S(2)}) async-start(bf16[32,2,512]{2,1,0:T(2,128)(2,1)} %reshape.39), calls=%async_computation.1 | async-start | bytes 131072 | tf_op jit(solution)/shard_map/all_to_all | solution.py:61
Sparse Core Ops, SparseCore 0:
  13.6 235.3 reduce-scatter.1
  252.1 80.0 all-gather.2
  335.9 71.8 all-gather.4
where the time goes:
time: 491 us; the launch traced here: 490 us
  waiting for transfers between devices  402 us (82%)
  blocking collectives  45.4 us (9%)
  between operations  13.9 us (3%)
  starting transfers between devices  9.81 us (2%)
  matrix products  7.7 us (2%)
  local copies, waits for them, and re-layouts  6.11 us (1%)
  other arithmetic  5.26 us (1%)
    reduce_scatter x1, waiting for transfers between devices, on_device(): lax.psum_scatter((picked * filled[:, None, None]).astype(jnp.bfloat16), '...  236 us
    all_gather x1, waiting for transfers between devices, on_device(): piece = lax.all_gather(summed, 'replica', axis=1, tiled=True)  83.2 us
    all_gather x1, waiting for transfers between devices, on_device(): lax.all_gather(left_product, 'replica', axis=1, tiled=True)  70.7 us
    psum x1, blocking collectives, on_device(): lax.psum((adam_squares, shaped_squares), 'replica')  45.4 us
    all_to_all x1, waiting for transfers between devices, on_device(): lax.all_to_all(direction, 'replica', split_axis=1, concat_axis=2, tiled=T...  11.8 us
  transfers between devices with their start and end apart: 4, of which 4 were waited for; matrix products, arithmetic and copies ran while one was open for 1% of the time, Pallas kernels for 0%

commit v1 on v0

v1 whole, which is shorter than its diff:
```python
import jax
import jax.numpy as jnp
from jax import lax
from jax.experimental import pallas as pl
from jax.experimental.pallas import tpu as pltpu
from jax.sharding import PartitionSpec as P

MESH = pl.DeviceIdType.MESH
NX, NY, NZ, NC = 4, 8, 16, 2
MOST, ROWS, WIDTH, BLOCKS = 4, 16, 512, 64
FAR = (4, 12, 8)
NEAR = (1, 15, 2)


def nt(a, b):
    return lax.dot_general(a, b, (((1,), (1,)), ((), ())), preferred_element_type=jnp.float32)


def nn(a, b):
    return lax.dot_general(a, b, (((1,), (0,)), ((), ())), preferred_element_type=jnp.float32)


def kernel(
    source, grads, left_stats, right_stats, moment, left_root, right_root,
    left_new, right_new, moment_new, direction,
    blocks, sendx, recvx, sendy, recvy, full, root, shaped, tally,
    load_sem, xs, xr, ys, yr, fs, fr, ns, nr, cs, cr, ts, tr,
):
    d, r = lax.axis_index("dp"), lax.axis_index("replica")
    x, y, z, c = d // NY, d % NY, r // NC, r % NC
    zhi, zlo = z // 4, z % 4

    def at(dx=0, dy=0, dz=0, dc=0):
        return (((x + dx) % NX) * NY + (y + dy) % NY, ((z + dz) % NZ) * NC + (c + dc) % NC)

    def copy(src, dst, s, e, target):
        return pltpu.make_async_remote_copy(
            src_ref=src, dst_ref=dst, send_sem=s, recv_sem=e, device_id=target, device_id_type=MESH
        )

    load = pltpu.make_async_copy(grads, blocks.at[pl.ds(0, BLOCKS)], load_sem.at[0])
    load.start()

    barrier = pltpu.get_barrier_semaphore()
    for i in range(1, NX):
        pl.semaphore_signal(barrier, inc=1, device_id=at(dx=i), device_id_type=MESH)
    for i in range(1, NY):
        pl.semaphore_signal(barrier, inc=1, device_id=at(dy=i), device_id_type=MESH)

    def greet(i, carry):
        pl.semaphore_signal(barrier, inc=1, device_id=at(dz=i // 2, dc=i % 2), device_id_type=MESH)
        return carry

    lax.fori_loop(1, NZ * NC, greet, 0)

    blocks[BLOCKS] = jnp.zeros((ROWS, WIDTH), jnp.bfloat16)
    root[:, zhi, zlo, c] = right_root[...]
    load.wait()

    def pick(k):
        def one(i, carry):
            to, row = i // NY, i % NY
            sendx[k, to, row] = blocks[source[(((x + to) % NX) * NY + row) * MOST + k]]
            return carry

        lax.fori_loop(0, NX * NY, one, 0)

    def x_copy(k, i):
        return copy(sendx.at[k, i], recvx.at[k, i - 1], xs.at[k, i - 1], xr.at[k, i - 1], at(dx=i))

    def x_send(k):
        for i in range(1, NX):
            x_copy(k, i).start()

    def x_sum(k):
        for i in range(1, NX):
            x_copy(k, i).wait_recv()

        def one(row, carry):
            total = sendx[k, 0, row].astype(jnp.float32)
            for i in range(NX - 1):
                total += recvx[k, i, row].astype(jnp.float32)
            sendy[k, row] = total.astype(jnp.bfloat16)
            return carry

        lax.fori_loop(0, NY, one, 0)

    def y_copy(k, i):
        return copy(
            sendy.at[k, (y + i) % NY], recvy.at[k, i - 1], ys.at[k, i - 1], yr.at[k, i - 1], at(dy=i)
        )

    def y_send(k):
        for i in range(1, NY):
            y_copy(k, i).start()

    def far_copy(ref, k, n, i):
        piece = ref.at[k, zhi, zlo, c]
        return copy(piece, piece, fs.at[n, i], fr.at[n, i], at(dz=FAR[i]))

    def near_copy(ref, k, n, i):
        piece = ref.at[k, :, zlo, c]
        return copy(piece, piece, ns.at[n, i], nr.at[n, i], at(dz=NEAR[i]))

    def twin_copy(ref, k, n, i):
        piece = ref.at[k, :, zlo, c] if i == 0 else ref.at[k, :, (z - NEAR[i - 1]) % 4, c]
        return copy(piece, piece, cs.at[n, i], cr.at[n, i], at(dc=1))

    def far(ref, k, n):
        for i in range(3):
            far_copy(ref, k, n, i).start()

    def near(ref, k, n):
        for i in range(3):
            far_copy(ref, k, n, i).wait_recv()
        for i in range(3):
            near_copy(ref, k, n, i).start()
        twin_copy(ref, k, n, 0).start()

    def twin(ref, k, n):
        for i in range(3):
            near_copy(ref, k, n, i).wait_recv()
            twin_copy(ref, k, n, i + 1).start()

    def gathered(ref, k, n):
        for i in range(4):
            twin_copy(ref, k, n, i).wait_recv()

    def y_sum(k):
        for i in range(1, NY):
            y_copy(k, i).wait_recv()
        total = sendy[k, y].astype(jnp.float32)
        for i in range(NY - 1):
            total += recvy[k, i].astype(jnp.float32)
        full[k, zhi, zlo, c] = total.astype(jnp.bfloat16)
        far(full, k, k)

    everything = pl.ds(0, MOST)
    lane = lax.broadcasted_iota(jnp.int32, (1, 128), 1)
    sums = jnp.zeros((1, 128), jnp.float32)

    pick(0)
    pl.semaphore_wait(barrier, NX - 1 + NY - 1 + NZ * NC - 1)
    x_send(0)
    far(root, everything, MOST)
    pick(1)
    x_send(1)
    pick(2)
    pick(3)
    x_sum(0)
    x_send(2)
    y_send(0)
    near(root, everything, MOST)
    x_sum(1)
    x_send(3)
    y_send(1)
    y_sum(0)
    x_sum(2)
    y_send(2)
    y_sum(1)
    near(full, 0, 0)
    twin(root, everything, MOST)
    x_sum(3)
    y_send(3)
    y_sum(2)
    near(full, 1, 1)
    y_sum(3)
    for k in range(MOST):
        wide = full[k, zhi, zlo, c].astype(jnp.float32)
        fresh = 0.95 * moment[k] + 0.05 * wide * wide
        moment_new[k] = fresh
        adam = wide / (jnp.sqrt(fresh) + 1e-08)
        sums += jnp.where(lane == k, jnp.sum(adam * adam), 0.0)
    twin(full, 0, 0)
    near(full, 2, 2)
    twin(full, 1, 1)
    near(full, 3, 3)

    base = z * (NC * ROWS) + c * ROWS
    chosen = lax.broadcasted_iota(jnp.int32, (ROWS, WIDTH), 1) == base + lax.broadcasted_iota(
        jnp.int32, (ROWS, WIDTH), 0
    )
    pick_cols = jnp.where(chosen, 1.0, 0.0).astype(jnp.bfloat16)

    gathered(root, everything, MOST)
    for k in range(MOST):
        if k >= 2:
            twin(full, k, k)
        gathered(full, k, k)
        block = full[k].reshape(WIDTH, WIDTH)
        across = nt(jnp.concatenate([full[k, zhi, zlo, c], pick_cols], axis=0), block)
        left_new[k] = 0.9 * left_stats[k] + 0.1 * across[:ROWS]
        own_cols = across[ROWS:].astype(jnp.bfloat16)
        down = nn(jnp.concatenate([left_root[k], own_cols], axis=0), block)
        right_new[k] = 0.9 * right_stats[k] + 0.1 * down[ROWS:]
        part = nn(down[:ROWS].astype(jnp.bfloat16), root[k].reshape(WIDTH, WIDTH))
        shaped[k] = part
        sums += jnp.where(lane == MOST + k, jnp.sum(part * part), 0.0)

    tally[0] = sums

    def tally_copy(i):
        return copy(
            tally.at[0], tally.at[i], ts.at[i - 1], tr.at[i - 1], at(dz=i // 2, dc=i % 2)
        )

    def tally_start(i, carry):
        tally_copy(i).start()
        return carry

    def tally_wait(i, carry):
        tally_copy(i).wait()
        return carry

    lax.fori_loop(1, NZ * NC, tally_start, 0)
    lax.fori_loop(1, NZ * NC, tally_wait, 0)
    totals = jnp.sum(tally[...], axis=0)
    entries = float(WIDTH * WIDTH)
    for k in range(MOST):
        adam_total = jnp.sum(jnp.where(lane == k, totals, 0.0), axis=1, keepdims=True)
        shaped_total = jnp.sum(jnp.where(lane == MOST + k, totals, 0.0), axis=1, keepdims=True)
        ratio = jnp.sqrt(adam_total / entries) / jnp.sqrt(shaped_total / entries + 1e-06)
        direction[k] = (shaped[k] * ratio).astype(jnp.bfloat16)

    for k in range(MOST):
        for i in range(1, NX):
            x_copy(k, i).wait_send()
        for i in range(1, NY):
            y_copy(k, i).wait_send()
    for ref, k, n in [(full, k, k) for k in range(MOST)] + [(root, everything, MOST)]:
        for i in range(3):
            far_copy(ref, k, n, i).wait_send()
            near_copy(ref, k, n, i).wait_send()
        for i in range(4):
            twin_copy(ref, k, n, i).wait_send()


def on_device(grads, assignment, left_stats, right_stats, second_moment, left_root, right_root):
    owner = assignment[:, 0]
    numbers = jnp.arange(BLOCKS, dtype=jnp.int32)
    same = (owner[:, None] == owner[None, :]) & (numbers[None, :] < numbers[:, None])
    slot = owner * MOST + jnp.sum(same.astype(jnp.int32), axis=1)
    slots = NX * NY * MOST
    match = (slot[:, None] == jnp.arange(slots, dtype=jnp.int32)[None, :]).astype(jnp.int32)
    source = BLOCKS + jnp.sum(match * (numbers[:, None] - BLOCKS), axis=0)

    vmem = pl.BlockSpec(memory_space=pltpu.VMEM)
    wide = jax.ShapeDtypeStruct((MOST, ROWS, WIDTH), jnp.float32)
    dma = pltpu.SemaphoreType.DMA
    gathers = MOST + 1
    return pl.pallas_call(
        kernel,
        name="shampoo",
        out_shape=[wide, wide, wide, jax.ShapeDtypeStruct((MOST, ROWS, WIDTH), jnp.bfloat16)],
        in_specs=[pl.BlockSpec(memory_space=pltpu.SMEM), pl.BlockSpec(memory_space=pl.ANY)] + [vmem] * 5,
        out_specs=[vmem] * 4,
        scratch_shapes=[
            pltpu.VMEM((BLOCKS + 1, ROWS, WIDTH), jnp.bfloat16),
            pltpu.VMEM((MOST, NX, NY, ROWS, WIDTH), jnp.bfloat16),
            pltpu.VMEM((MOST, NX - 1, NY, ROWS, WIDTH), jnp.bfloat16),
            pltpu.VMEM((MOST, NY, ROWS, WIDTH), jnp.bfloat16),
            pltpu.VMEM((MOST, NY - 1, ROWS, WIDTH), jnp.bfloat16),
            pltpu.VMEM((MOST, 4, 4, NC, ROWS, WIDTH), jnp.bfloat16),
            pltpu.VMEM((MOST, 4, 4, NC, ROWS, WIDTH), jnp.bfloat16),
            pltpu.VMEM((MOST, ROWS, WIDTH), jnp.float32),
            pltpu.VMEM((NZ * NC, 1, 128), jnp.float32),
            dma((1,)),
            dma((MOST, NX - 1)),
            dma((MOST, NX - 1)),
            dma((MOST, NY - 1)),
            dma((MOST, NY - 1)),
            dma((gathers, 3)),
            dma((gathers, 3)),
            dma((gathers, 3)),
            dma((gathers, 3)),
            dma((gathers, 4)),
            dma((gathers, 4)),
            dma((NZ * NC - 1,)),
            dma((NZ * NC - 1,)),
        ],
        compiler_params=pltpu.CompilerParams(
            collective_id=0, has_side_effects=True, vmem_limit_bytes=32 << 20
        ),
        cost_estimate=pl.CostEstimate(flops=140_000_000, bytes_accessed=2_400_000, transcendentals=70_000),
    )(source, grads[0], left_stats, right_stats, second_moment, left_root, right_root)


def solution(mesh):
    rows = P("dp", "replica", None)
    return jax.shard_map(
        on_device,
        mesh=mesh,
        in_specs=(P("dp", None, "replica", None), P(), rows, rows, rows, rows, rows),
        out_specs=(rows,) * 4,
        check_vma=False,
    )
```

time: 491 us -> 111 us (0.23)
  waiting for transfers between devices: 402 us -> 0 us
  Pallas kernels: 0 us -> 101 us
  blocking collectives: 45.4 us -> 0 us
  between operations: 13.9 us -> 0.68 us
  starting transfers between devices: 9.81 us -> 0 us
  matrix products: 7.7 us -> 0 us
  other arithmetic: 5.26 us -> 0.29 us
    reduce_scatter x1 -> x0, waiting for transfers between devices: 236 us -> none  [on_device(): lax.psum_scatter((picked * filled[:, None, None]).astype(jnp.bfloat16), '...]
    all_gather x2 -> x0, waiting for transfers between devices: 154 us -> none  [the longest x1 83.2 us: on_device(): piece = lax.all_gather(summed, 'replica', axis=1, tiled=True)]
    pallas_call x0 -> x1, Pallas kernels: none -> 101 us  [on_device(): pl.pallas_call(kernel, name='shampoo', out_shape=[wide, wide, wide, jax.S...]
    psum x1 -> x0, blocking collectives: 45.4 us -> none  [on_device(): lax.psum((adam_squares, shaped_squares), 'replica')]
    all_to_all x1 -> x0, waiting for transfers between devices: 11.8 us -> none  [on_device(): lax.all_to_all(direction, 'replica', split_axis=1, concat_axis=2, tiled=T...]
    all_to_all x1 -> x0, starting transfers between devices: 9.69 us -> none  [on_device(): lax.all_to_all(direction, 'replica', split_axis=1, concat_axis=2, tiled=T...]
    dot_general x4 -> x0, matrix products: 7.7 us -> none  [the longest x1 2.76 us: on_device(): jnp.einsum('kij,kjb->kib', left_root, piece, preferred_element_type=jnp.f...]
    unnamed x16 -> x18, local copies, waits for them, and re-layouts: 2.64 us -> 8.85 us
  transfers between devices with their start and end apart: 4 -> 0, of which waited for: 4 -> 0; matrix products, arithmetic and copies ran while one was open for 1% -> 0% of each run, Pallas kernels for 0% -> 0%
where the time goes in v1:
time: 111 us
  Pallas kernels  101 us (91%)
  local copies, waits for them, and re-layouts  8.85 us (8%)
    pallas_call x1, Pallas kernels, on_device(): pl.pallas_call(kernel, name='shampoo', out_shape=[wide, wide, wide, jax.S...  101 us
    unnamed x18, local copies, waits for them, and re-layouts  8.85 us

profile of v1, /device:TPU:1, one launch (start us, length us, event | category | flops | bytes accessed | tf_op | source)
XLA Modules:
  0.0 110.8 jit_solution(6230637431717513191)
XLA Ops:
  0.6 0.0 copy-start.6
  0.6 0.6 copy-done.6
  1.3 0.2 convert_reduce_fusion
  1.5 0.1 select_reduce_fusion
  1.6 0.0 copy-start
  1.6 1.2 %copy-done = bf16[1,64,16,512]{3,2,1,0:T(8,128)(2,1)S(1)} copy-done((bf16[1,64,16,512]{3,2,1,0:T(8,128)(2,1)S(1)}, bf16[1,64,16,512]{3,2,1,0:T(8,128)(2,1)}, u32[]{:S(2)}) %copy-start) | copy-done | bytes 1048600
  2.8 0.0 copy-start.1
  2.8 0.9 copy-done.1
  3.7 0.0 copy-start.2
  3.7 0.9 copy-done.2
  4.6 0.0 copy-start.3
  4.6 0.9 copy-done.3
  5.5 0.0 copy-start.4
  5.5 0.8 copy-done.4
  6.4 0.0 copy-start.5
  6.4 0.8 copy-done.5
  7.2 101.0 %shampoo.1 = (f32[4,16,512]{2,1,0:T(8,128)S(1)}, f32[4,16,512]{2,1,0:T(8,128)S(1)}, f32[4,16,512]{2,1,0:T(8,128)S(1)}, bf16[4,16,512]{2,1,0:T(8,128)(2,1)S(1)}) custom-call(s32[128]{0:T(128)S(1)} %broadcast_add_fusion.source, bf16[64,16,512]{2,1,0:T(8,128)(2,1)S(1)} %bitcast.8, f32[4,16,512]{2,1,0:T(8,128)S(1)} %copy-done.1, f32[4,16,512]{2,1,0:T(8,128)S(1)} %copy-done.2, ...), custom_call_target="tpu_custom_call" | custom-call | flops 140000000 | bytes 2400000 | tf_op jit(solution)/shard_map/shampoo/pallas_call | solution.py:251
  108.2 0.7 copy.15
  108.8 0.7 copy.16
  109.5 0.7 copy.17
  110.2 0.6 copy.18
  (3 shorter events, 0.0 us)
Async XLA Ops:
  0.6 0.7 copy-start.6
  1.6 1.2 %copy-start = (bf16[1,64,16,512]{3,2,1,0:T(8,128)(2,1)S(1)}, bf16[1,64,16,512]{3,2,1,0:T(8,128)(2,1)}, u32[]{:S(2)}) copy-start(bf16[1,64,16,512]{3,2,1,0:T(8,128)(2,1)} %param.7) | copy-start | bytes 3145732
  2.8 0.9 copy-start.1
  3.7 0.9 copy-start.2
  4.6 0.9 copy-start.3
  5.5 0.8 copy-start.4
  6.4 0.8 copy-start.5

commit v2 on v1

v2 whole, which is shorter than its diff:
```python
import jax
import jax.numpy as jnp
from jax import lax
from jax.experimental import pallas as pl
from jax.experimental.pallas import tpu as pltpu
from jax.sharding import PartitionSpec as P

MESH = pl.DeviceIdType.MESH
NX, NY, NZ, NC = 4, 8, 16, 2
MOST, ROWS, WIDTH, BLOCKS = 4, 16, 512, 64
XFIRST = 3
NEAR = (0, -1, 1, 2)


def nt(a, b):
    return lax.dot_general(a, b, (((1,), (1,)), ((), ())), preferred_element_type=jnp.float32)


def nn(a, b):
    return lax.dot_general(a, b, (((1,), (0,)), ((), ())), preferred_element_type=jnp.float32)


def kernel(
    source, grads, left_stats, right_stats, moment, left_root, right_root,
    left_new, right_new, moment_new, direction,
    blocks, stats, mine, sendx, recvx, sendy, recvy, sendq, recvq, sendr, recvr,
    low, full, roots, outbox, inbox, norms, tally,
    load_sem, xs, xr, ys, yr, qs, qr, ps, pr, rs, rr, us, ur, gs, gr, cs, cr, ns, nr, ms, mr, ts, tr,
):
    d, r = lax.axis_index("dp"), lax.axis_index("replica")
    x, y, z, c = d // NY, d % NY, r // NC, r % NC

    def at(dx=0, dy=0, dz=0, dc=0):
        return (((x + dx) % NX) * NY + (y + dy) % NY, ((z + dz) % NZ) * NC + (c + dc) % NC)

    def copy(src, dst, s, e, target):
        return pltpu.make_async_remote_copy(
            src_ref=src, dst_ref=dst, send_sem=s, recv_sem=e, device_id=target, device_id_type=MESH
        )

    def loop(start, stop, body):
        def step(i, carry):
            body(i)
            return carry

        lax.fori_loop(start, stop, step, 0)

    loads = [
        pltpu.make_async_copy(a, b, load_sem.at[i])
        for i, (a, b) in enumerate((
            (grads, blocks.at[pl.ds(0, BLOCKS)]),
            (left_root, mine.at[:, 0]),
            (right_root, mine.at[:, 1]),
            (moment, stats.at[2]),
            (left_stats, stats.at[0]),
            (right_stats, stats.at[1]),
        ))
    ]
    for load in loads:
        load.start()

    barrier = pltpu.get_barrier_semaphore()
    for i in range(1, NX):
        pl.semaphore_signal(barrier, inc=1, device_id=at(dx=i), device_id_type=MESH)
    for i in range(1, NY):
        pl.semaphore_signal(barrier, inc=1, device_id=at(dy=i), device_id_type=MESH)
    loop(1, NZ * NC, lambda i: pl.semaphore_signal(
        barrier, inc=1, device_id=at(dz=i // 2, dc=i % 2), device_id_type=MESH
    ))

    blocks[BLOCKS] = jnp.zeros((ROWS, WIDTH), jnp.bfloat16)


    def pick(k):
        def one(i):
            to, row = i // NY, i % NY
            sendx[k, to, row] = blocks[source[(((x + to) % NX) * NY + row) * MOST + k]]

        loop(0, NX * NY, one)

    def x_copy(k, i):
        return copy(sendx.at[k, i], recvx.at[k, i - 1], xs.at[k, i - 1], xr.at[k, i - 1], at(dx=i))

    def x_send(k):
        for i in range(1, NX):
            x_copy(k, i).start()

    def x_sum(k):
        for i in range(1, NX):
            x_copy(k, i).wait_recv()

        def one(row):
            total = sendx[k, 0, row].astype(jnp.float32)
            for i in range(NX - 1):
                total += recvx[k, i, row].astype(jnp.float32)
            sendy[k, row] = total.astype(jnp.bfloat16)

        loop(0, NY, one)

    def y_copy(k, i):
        return copy(
            sendy.at[k, (y + i) % NY], recvy.at[k, i - 1], ys.at[k, i - 1], yr.at[k, i - 1], at(dy=i)
        )

    def y_send(k):
        for i in range(1, NY):
            y_copy(k, i).start()

    def y_sum(k):
        for i in range(1, NY):
            y_copy(k, i).wait_recv()
        total = sendy[k, y].astype(jnp.float32)
        for i in range(NY - 1):
            total += recvy[k, i].astype(jnp.float32)
        low[k] = total.astype(jnp.bfloat16)


    def pick_last():
        def one(i):
            to, row = i // NX, i % NX
            sendq[to, row] = blocks[source[(row * NY + (y + to) % NY) * MOST + XFIRST]]

        loop(0, NX * NY, one)

    def q_copy(i):
        return copy(sendq.at[i], recvq.at[i - 1], qs.at[i - 1], qr.at[i - 1], at(dy=i))

    def q_sum():
        for i in range(1, NY):
            q_copy(i).wait_recv()

        def one(row):
            total = sendq[0, row].astype(jnp.float32)
            for i in range(NY - 1):
                total += recvq[i, row].astype(jnp.float32)
            sendr[row] = total.astype(jnp.bfloat16)

        loop(0, NX, one)

    def p_copy(i):
        return copy(sendr.at[(x + i) % NX], recvr.at[i - 1], ps.at[i - 1], pr.at[i - 1], at(dx=i))

    def p_sum():
        for i in range(1, NX):
            p_copy(i).wait_recv()
        total = sendr[x].astype(jnp.float32)
        for i in range(NX - 1):
            total += recvr[i].astype(jnp.float32)
        low[XFIRST] = total.astype(jnp.bfloat16)


    def root_copy(dz):
        return copy(mine.at[(z + dz) % MOST], roots.at[:, z, c], rs.at[dz], rr.at[dz], at(dz=dz))

    def root_relay():
        lane = roots.at[:, :, c]
        return copy(lane, lane, us.at[0], ur.at[0], at(dc=1))

    def g_copy(k, dz):
        return copy(low.at[k], full.at[z, c], gs.at[dz], gr.at[dz], at(dz=dz))

    def g_send(k):
        first = (k - z) % MOST
        for j in range(1, NZ // MOST):
            g_copy(k, first + j * MOST).start()

        @pl.when(first != 0)
        def _():
            g_copy(k, first).start()

        @pl.when(first == 0)
        def _():
            full[z, c] = low[k]

    def g_relay(dz):
        piece = full.at[(z - dz) % NZ, c]
        return copy(piece, piece, cs.at[dz], cr.at[dz], at(dc=1))

    def g_pass(dz):
        g_copy(0, dz).wait_recv()
        g_relay(dz).start()

    def tally_copy(i):
        return copy(tally.at[0], tally.at[i], ts.at[i - 1], tr.at[i - 1], at(dz=i // 2, dc=i % 2))

    def near_copy(i):
        return copy(outbox.at[i], inbox.at[i], ns.at[i - 1], nr.at[i - 1], at(dz=NEAR[i]))

    def norm_copy(i):
        return copy(norms.at[0], norms.at[i], ms.at[i - 1], mr.at[i - 1], at(dz=NEAR[i]))

    loads[0].wait()
    pick(0)
    pick_last()
    pl.semaphore_wait(barrier, NX - 1 + NY - 1 + NZ * NC - 1)
    x_send(0)
    for i in range(1, NY):
        q_copy(i).start()
    loads[1].wait()
    loads[2].wait()
    loop(1, NZ, lambda dz: root_copy(dz).start())
    pick(1)
    x_send(1)
    roots[:, z, c] = mine[z % MOST]
    pick(2)
    x_sum(0)
    x_send(2)
    y_send(0)
    x_sum(1)
    y_send(1)
    q_sum()
    for i in range(1, NX):
        p_copy(i).start()
    y_sum(0)
    g_send(0)
    x_sum(2)
    y_send(2)
    p_sum()
    g_send(3)
    y_sum(1)
    g_send(1)
    y_sum(2)
    g_send(2)

    lane = lax.broadcasted_iota(jnp.int32, (1, 128), 1)
    sums = jnp.zeros((1, 128), jnp.float32)
    for load in loads[3:]:
        load.wait()
    for k in range(MOST):
        wide = low[k].astype(jnp.float32)
        fresh = 0.95 * stats[2, k] + 0.05 * wide * wide
        moment_new[k] = fresh
        adam = wide / (jnp.sqrt(fresh) + 1e-08)
        sums += jnp.where(lane == k, jnp.sum(adam * adam), 0.0)
    tally[0] = sums
    loop(1, NZ * NC, lambda i: tally_copy(i).start())

    loop(1, NZ, lambda dz: root_copy(dz).wait_recv())
    root_relay().start()
    g_relay(0).start()
    loop(1, NZ, g_pass)

    chosen = []
    for i in NEAR:
        base = ((z + i) % NZ) * (NC * ROWS) + c * ROWS
        rows = lax.broadcasted_iota(jnp.int32, (ROWS, WIDTH), 0) + base
        hit = lax.broadcasted_iota(jnp.int32, (ROWS, WIDTH), 1) == rows
        chosen.append(jnp.where(hit, 1.0, 0.0).astype(jnp.bfloat16))

    root_relay().wait_recv()
    loop(0, NZ, lambda dz: g_relay(dz).wait_recv())

    many = len(NEAR) * ROWS
    block = full[...].reshape(WIDTH, WIDTH)
    right = roots[1].reshape(WIDTH, WIDTH)
    across = nt(jnp.concatenate([full[(z + i) % NZ, c] for i in NEAR] + chosen, axis=0), block)
    cols = across[many:].astype(jnp.bfloat16)
    down = nn(
        jnp.concatenate([roots[0, (z + i) % NZ, c] for i in NEAR] + [cols], axis=0), block
    )
    part = nn(down[:many].astype(jnp.bfloat16), right)
    for i in range(len(NEAR)):
        at_i = slice(i * ROWS, (i + 1) * ROWS)
        box = inbox if i == 0 else outbox
        box[i, 0] = across[at_i].astype(jnp.bfloat16)
        box[i, 1] = down[many + i * ROWS:many + (i + 1) * ROWS].astype(jnp.bfloat16)
        box[i, 2] = part[at_i].astype(jnp.bfloat16)
        if i > 0:
            near_copy(i).start()

    squares = jnp.zeros((1, 1), jnp.float32)
    for i in range(2):
        half = roots[0, i * 8:(i + 1) * 8].reshape(WIDTH // 2, WIDTH)
        shaped = nn(nn(half, block).astype(jnp.bfloat16), right)
        squares += jnp.sum(shaped * shaped).reshape(1, 1)
    norms[0] = jnp.broadcast_to(squares, (1, 128))
    for i in range(1, len(NEAR)):
        norm_copy(i).start()

    for i in range(len(NEAR)):
        if i > 0:
            near_copy(i).wait_recv()
        k = (z - NEAR[i]) % MOST
        left_new[k] = 0.9 * stats[0, k] + 0.1 * inbox[i, 0].astype(jnp.float32)
        right_new[k] = 0.9 * stats[1, k] + 0.1 * inbox[i, 1].astype(jnp.float32)

    loop(1, NZ * NC, lambda i: tally_copy(i).wait())
    totals = jnp.sum(tally[...], axis=0)
    entries = float(WIDTH * WIDTH)
    for i in range(len(NEAR)):
        if i > 0:
            norm_copy(i).wait_recv()
        k = (z - NEAR[i]) % MOST
        adam_total = jnp.sum(jnp.where(lane == k, totals, 0.0), axis=1, keepdims=True)
        ratio = jnp.sqrt(adam_total / entries) / jnp.sqrt(norms[i][:, :1] / entries + 1e-06)
        direction[k] = (inbox[i, 2].astype(jnp.float32) * ratio).astype(jnp.bfloat16)

    for k in range(XFIRST):
        for i in range(1, NX):
            x_copy(k, i).wait_send()
        for i in range(1, NY):
            y_copy(k, i).wait_send()
    for i in range(1, NY):
        q_copy(i).wait_send()
    for i in range(1, NX):
        p_copy(i).wait_send()
    root_relay().wait_send()
    g_relay(0).wait_send()

    def sent(dz):
        root_copy(dz).wait_send()
        g_copy(0, dz).wait_send()
        g_relay(dz).wait_send()

    loop(1, NZ, sent)
    for i in range(1, len(NEAR)):
        near_copy(i).wait_send()
        norm_copy(i).wait_send()


def on_device(grads, assignment, left_stats, right_stats, second_moment, left_root, right_root):
    owner = assignment[:, 0]
    numbers = jnp.arange(BLOCKS, dtype=jnp.int32)
    same = (owner[:, None] == owner[None, :]) & (numbers[None, :] < numbers[:, None])
    slot = owner * MOST + jnp.sum(same.astype(jnp.int32), axis=1)
    slots = NX * NY * MOST
    match = (slot[:, None] == jnp.arange(slots, dtype=jnp.int32)[None, :]).astype(jnp.int32)
    source = BLOCKS + jnp.sum(match * (numbers[:, None] - BLOCKS), axis=0)

    wide = jax.ShapeDtypeStruct((MOST, ROWS, WIDTH), jnp.float32)
    narrow = jnp.bfloat16
    dma = pltpu.SemaphoreType.DMA
    tile = (ROWS, WIDTH)
    near = len(NEAR)

    def pair(*shape):
        return [dma(shape), dma(shape)]

    return pl.pallas_call(
        kernel,
        name="shampoo",
        out_shape=[wide, wide, wide, jax.ShapeDtypeStruct((MOST, ROWS, WIDTH), narrow)],
        in_specs=[pl.BlockSpec(memory_space=pltpu.SMEM)] + [pl.BlockSpec(memory_space=pl.ANY)] * 6,
        out_specs=[pl.BlockSpec(memory_space=pltpu.VMEM)] * 4,
        scratch_shapes=[
            pltpu.VMEM((BLOCKS + 1, *tile), narrow),
            pltpu.VMEM((3, MOST, *tile), jnp.float32),
            pltpu.VMEM((MOST, 2, *tile), narrow),
            pltpu.VMEM((XFIRST, NX, NY, *tile), narrow),
            pltpu.VMEM((XFIRST, NX - 1, NY, *tile), narrow),
            pltpu.VMEM((XFIRST, NY, *tile), narrow),
            pltpu.VMEM((XFIRST, NY - 1, *tile), narrow),
            pltpu.VMEM((NY, NX, *tile), narrow),
            pltpu.VMEM((NY - 1, NX, *tile), narrow),
            pltpu.VMEM((NX, *tile), narrow),
            pltpu.VMEM((NX - 1, *tile), narrow),
            pltpu.VMEM((MOST, *tile), narrow),
            pltpu.VMEM((NZ, NC, *tile), narrow),
            pltpu.VMEM((2, NZ, NC, *tile), narrow),
            pltpu.VMEM((near, 3, *tile), narrow),
            pltpu.VMEM((near, 3, *tile), narrow),
            pltpu.VMEM((near, 1, 128), jnp.float32),
            pltpu.VMEM((NZ * NC, 1, 128), jnp.float32),
            dma((6,)),
            *pair(XFIRST, NX - 1),
            *pair(XFIRST, NY - 1),
            *pair(NY - 1),
            *pair(NX - 1),
            *pair(NZ),
            *pair(1),
            *pair(NZ),
            *pair(NZ),
            *pair(near - 1),
            *pair(near - 1),
            *pair(NZ * NC - 1),
        ],
        compiler_params=pltpu.CompilerParams(
            collective_id=0, has_side_effects=True, vmem_limit_bytes=56 << 20
        ),
        cost_estimate=pl.CostEstimate(flops=800_000_000, bytes_accessed=2_400_000, transcendentals=70_000),
    )(source, grads[0], left_stats, right_stats, second_moment, left_root, right_root)


def solution(mesh):
    rows = P("dp", "replica", None)
    return jax.shard_map(
        on_device,
        mesh=mesh,
        in_specs=(P("dp", None, "replica", None), P(), rows, rows, rows, rows, rows),
        out_specs=(rows,) * 4,
        check_vma=False,
    )
```

time: 111 us -> 80.5 us (0.73)
  Pallas kernels: 101 us -> 74.1 us
  local copies, waits for them, and re-layouts: 8.85 us -> 4.7 us
    pallas_call x1, Pallas kernels: 101 us -> 74.1 us  [on_device(): pl.pallas_call(kernel, name='shampoo', out_shape=[wide, wide, wide, jax.S...]
    unnamed x18 -> x12, local copies, waits for them, and re-layouts: 8.85 us -> 4.7 us
where the time goes in v2:
time: 80.5 us; the launch traced here: 80.2 us
  Pallas kernels  74.1 us (92%)
  local copies, waits for them, and re-layouts  4.7 us (6%)
    pallas_call x1, Pallas kernels, on_device(): pl.pallas_call(kernel, name='shampoo', out_shape=[wide, wide, wide, jax.S...  74.1 us
    unnamed x12, local copies, waits for them, and re-layouts  4.7 us

profile of v2, /device:TPU:1, one launch (start us, length us, event | category | flops | bytes accessed | tf_op | source)
XLA Modules:
  0.0 80.2 jit_solution(17139632186977586416)
XLA Ops:
  0.6 0.0 copy-start.3
  0.6 0.6 copy-done.3
  1.3 0.2 convert_reduce_fusion
  1.5 0.1 select_reduce_fusion
  1.6 0.5 broadcast_add_fusion.source
  2.1 74.1 %shampoo.1 = (f32[4,16,512]{2,1,0:T(8,128)}, f32[4,16,512]{2,1,0:T(8,128)}, f32[4,16,512]{2,1,0:T(8,128)}, bf16[4,16,512]{2,1,0:T(8,128)(2,1)}) custom-call(s32[128]{0:T(128)} %broadcast_add_fusion.source, bf16[64,16,512]{2,1,0:T(8,128)(2,1)} %bitcast.8, f32[4,16,512]{2,1,0:T(8,128)} %left_stats.1, f32[4,16,512]{2,1,0:T(8,128)} %right_stats.1, ...), custom_call_target="tpu_custom_call" | custom-call | flops 800000000 | bytes 2400000 | tf_op jit(solution)/shard_map/shampoo/pallas_call | solution.py:339
  76.2 0.0 copy-start.1
  76.2 1.6 %copy.15 = f32[4,16,512]{2,1,0:T(8,128)} copy(f32[4,16,512]{2,1,0:T(8,128)} %get-tuple-element.8) | data formatting | bytes 262144
  77.8 0.0 copy-done.1
  77.8 0.0 copy-start
  77.8 0.7 copy.16
  78.4 0.3 copy-done
  78.7 0.0 copy-start.2
  78.7 0.7 copy.17
  79.4 0.2 copy-done.2
  79.6 0.6 copy.18
  (2 shorter events, 0.0 us)
Async XLA Ops:
  0.6 0.7 copy-start.3
  76.2 1.6 %copy-start.1 = (f32[4,16,512]{2,1,0:T(8,128)S(1)}, f32[4,16,512]{2,1,0:T(8,128)}, u32[]{:S(2)}) copy-start(f32[4,16,512]{2,1,0:T(8,128)} %get-tuple-element.9) | copy-start | bytes 393220
  77.8 1.0 %copy-start = (f32[4,16,512]{2,1,0:T(8,128)S(1)}, f32[4,16,512]{2,1,0:T(8,128)}, u32[]{:S(2)}) copy-start(f32[4,16,512]{2,1,0:T(8,128)} %get-tuple-element.10) | copy-start | bytes 393220
  78.7 0.9 %copy-start.2 = (bf16[4,16,512]{2,1,0:T(8,128)(2,1)S(1)}, bf16[4,16,512]{2,1,0:T(8,128)(2,1)}, u32[]{:S(2)}) copy-start(bf16[4,16,512]{2,1,0:T(8,128)(2,1)} %get-tuple-element.11) | copy-start | bytes 196612

commit v3 on v2

v3 whole, which is shorter than its diff:
```python
import functools

import jax
import jax.numpy as jnp
from jax import lax
from jax.experimental import pallas as pl
from jax.experimental.pallas import tpu as pltpu
from jax.sharding import PartitionSpec as P

MESH = pl.DeviceIdType.MESH
NX, NY, NZ, NC = 4, 8, 16, 2
MOST, ROWS, WIDTH, BLOCKS = 4, 16, 512, 64
XFIRST = 2
REST = MOST - XFIRST
CROWD = REST * NX
NEAR = (0, -1, 1, 2)


def nt(a, b):
    return lax.dot_general(a, b, (((1,), (1,)), ((), ())), preferred_element_type=jnp.float32)


def nn(a, b):
    return lax.dot_general(a, b, (((1,), (0,)), ((), ())), preferred_element_type=jnp.float32)


def kernel(
    cap, table, grads, left_stats, right_stats, moment, left_root, right_root,
    left_new, right_new, moment_new, direction,
    fresh, turned, blocks, stats, mine, sendx, recvx, sendy, recvy, sendq, recvq, crowd, sendr, recvr,
    low, full, roots, lefts, outbox, inbox, pair, tally,
    load_sem, save_sem, xs, xr, ys, yr, qs, qr, ps, pr, rs, rr, us, ur, gs, gr, cs, cr, ns, nr, ls, lr, vs, vr, ts, tr,
):
    d, r = lax.axis_index("dp"), lax.axis_index("replica")
    x, y, z, c = d // NY, d % NY, r // NC, r % NC

    def at(dx=0, dy=0, dz=0, dc=0):
        return (((x + dx) % NX) * NY + (y + dy) % NY, ((z + dz) % NZ) * NC + (c + dc) % NC)

    def copy(src, dst, s, e, target):
        return pltpu.make_async_remote_copy(
            src_ref=src, dst_ref=dst, send_sem=s, recv_sem=e, device_id=target, device_id_type=MESH
        )

    def loop(start, stop, body):
        def step(i, carry):
            body(i)
            return carry

        lax.fori_loop(start, stop, step, 0)

    loads = [
        pltpu.make_async_copy(a, b, load_sem.at[i])
        for i, (a, b) in enumerate((
            (grads, blocks.at[pl.ds(0, BLOCKS)]),
            (left_root, mine.at[0]),
            (right_root, mine.at[1]),
            (moment, stats.at[2]),
            (left_stats, stats.at[0]),
            (right_stats, stats.at[1]),
        ))
    ]
    for load in loads:
        load.start()

    saves = [
        pltpu.make_async_copy(a, b, save_sem.at[i])
        for i, (a, b) in enumerate((
            (fresh.at[0], left_new),
            (fresh.at[1], right_new),
            (fresh.at[2], moment_new),
            (turned, direction),
        ))
    ]

    barrier = pltpu.get_barrier_semaphore()
    for i in range(1, NX):
        pl.semaphore_signal(barrier, inc=1, device_id=at(dx=i), device_id_type=MESH)
    for i in range(1, NY):
        pl.semaphore_signal(barrier, inc=1, device_id=at(dy=i), device_id_type=MESH)
    loop(1, NZ, lambda i: pl.semaphore_signal(
        barrier, inc=1, device_id=at(dz=i), device_id_type=MESH
    ))
    pl.semaphore_signal(barrier, inc=1, device_id=at(dc=1), device_id_type=MESH)

    blocks[BLOCKS] = jnp.zeros((ROWS, WIDTH), jnp.bfloat16)
    crowd[CROWD] = jnp.zeros((ROWS, WIDTH), jnp.bfloat16)


    def pick(k):
        def one(i):
            to, row = i // NY, i % NY
            sendx[k, to, row] = blocks[table[(((x + to) % NX) * NY + row) * XFIRST + k]]

        loop(0, NX * NY, one)

    def x_copy(k, i):
        return copy(sendx.at[k, i], recvx.at[k, i - 1], xs.at[k, i - 1], xr.at[k, i - 1], at(dx=i))

    def x_send(k):
        for i in range(1, NX):
            x_copy(k, i).start()

    def x_sum(k):
        for i in range(1, NX):
            x_copy(k, i).wait_recv()

        def one(row):
            total = sendx[k, 0, row].astype(jnp.float32)
            for i in range(NX - 1):
                total += recvx[k, i, row].astype(jnp.float32)
            sendy[k, row] = total.astype(jnp.bfloat16)

        loop(0, NY, one)

    def y_copy(k, i):
        return copy(
            sendy.at[k, (y + i) % NY], recvy.at[k, i - 1], ys.at[k, i - 1], yr.at[k, i - 1], at(dy=i)
        )

    def y_send(k):
        for i in range(1, NY):
            y_copy(k, i).start()

    def y_sum(k):
        for i in range(1, NY):
            y_copy(k, i).wait_recv()
        total = sendy[k, y].astype(jnp.float32)
        for i in range(NY - 1):
            total += recvy[k, i].astype(jnp.float32)
        low[k] = total.astype(jnp.bfloat16)


    def pick_last():
        def one(i):
            to, row = i // cap, i % cap
            sendq[to, row] = blocks[table[BLOCKS + ((y + to) % NY) * CROWD + row]]

        loop(0, NY * cap, one)

    def q_copy(i):
        return copy(sendq.at[i], recvq.at[i - 1], qs.at[i - 1], qr.at[i - 1], at(dy=i))

    def q_sum():
        for i in range(1, NY):
            q_copy(i).wait_recv()

        def one(row):
            total = sendq[0, row].astype(jnp.float32)
            for i in range(NY - 1):
                total += recvq[i, row].astype(jnp.float32)
            crowd[row] = total.astype(jnp.bfloat16)

        loop(0, cap, one)

        def spread(i):
            to, row = i // REST, i % REST
            sendr[to, row] = crowd[table[2 * BLOCKS + (to * NY + y) * REST + row]]

        loop(0, NX * REST, spread)

    def p_copy(i):
        return copy(sendr.at[(x + i) % NX], recvr.at[i - 1], ps.at[i - 1], pr.at[i - 1], at(dx=i))

    def p_sum():
        for i in range(1, NX):
            p_copy(i).wait_recv()
        total = sendr[x].astype(jnp.float32)
        for i in range(NX - 1):
            total += recvr[i].astype(jnp.float32)
        low[pl.ds(XFIRST, REST)] = total.astype(jnp.bfloat16)


    def root_copy(dz):
        return copy(mine.at[1, (z + dz) % MOST], roots.at[z, c], rs.at[dz], rr.at[dz], at(dz=dz))

    def root_relay():
        lane = roots.at[:, c]
        return copy(lane, lane, us.at[0], ur.at[0], at(dc=1))

    def g_copy(k, dz):
        return copy(low.at[k], full.at[z, c], gs.at[dz], gr.at[dz], at(dz=dz))

    def g_send(k):
        first = (k - z) % MOST
        for j in range(1, NZ // MOST):
            g_copy(k, first + j * MOST).start()

        @pl.when(first != 0)
        def _():
            g_copy(k, first).start()

        @pl.when(first == 0)
        def _():
            full[z, c] = low[k]

    def g_relay():
        lane = full.at[:, c]
        return copy(lane, lane, cs.at[0], cr.at[0], at(dc=1))

    def tally_copy(i):
        return copy(tally.at[0], tally.at[i], ts.at[i], tr.at[i], at(dz=i))

    def pair_copy():
        return copy(pair.at[0], pair.at[1], ts.at[0], tr.at[0], at(dc=1))

    def near_copy(i):
        return copy(outbox.at[i], inbox.at[i], ns.at[i - 1], nr.at[i - 1], at(dz=NEAR[i]))

    def left_copy(i):
        return copy(
            mine.at[0, (z - NEAR[i]) % MOST], lefts.at[i, c], ls.at[i - 1], lr.at[i - 1], at(dz=-NEAR[i])
        )

    def left_relay():
        piece = lefts.at[:, c]
        return copy(piece, piece, vs.at[0], vr.at[0], at(dc=1))

    loads[0].wait()
    pick(0)
    pick_last()
    pl.semaphore_wait(barrier, NX - 1 + NY - 1 + NZ - 1 + NC - 1)
    x_send(0)
    for i in range(1, NY):
        q_copy(i).start()
    pick(1)
    x_send(1)
    loads[1].wait()
    loads[2].wait()
    loop(1, NZ, lambda dz: root_copy(dz).start())
    roots[z, c] = mine[1, z % MOST]
    lefts[0, c] = mine[0, z % MOST]
    for i in range(1, len(NEAR)):
        left_copy(i).start()
    x_sum(0)
    y_send(0)
    x_sum(1)
    y_send(1)
    y_sum(0)
    g_send(0)
    q_sum()
    for i in range(1, NX):
        p_copy(i).start()
    for i in range(1, len(NEAR)):
        left_copy(i).wait()
    left_relay().start()
    y_sum(1)
    g_send(1)
    p_sum()
    g_send(2)
    g_send(3)
    loop(1, NZ, lambda dz: root_copy(dz).wait_recv())
    root_relay().start()

    lane = lax.broadcasted_iota(jnp.int32, (1, 128), 1)
    sums = jnp.zeros((1, 128), jnp.float32)
    for load in loads[3:]:
        load.wait()
    for k in range(MOST):
        wide = low[k].astype(jnp.float32)
        second = 0.95 * stats[2, k] + 0.05 * wide * wide
        fresh[2, k] = second
        adam = wide / (jnp.sqrt(second) + 1e-08)
        sums += jnp.where(lane == k, jnp.sum(adam * adam), 0.0)
    saves[2].start()
    pair[0] = sums
    pair_copy().start()
    for k in range(XFIRST):
        for i in range(1, NX):
            x_copy(k, i).wait_send()
        for i in range(1, NY):
            y_copy(k, i).wait_send()
    for i in range(1, NY):
        q_copy(i).wait_send()
    for i in range(1, NX):
        p_copy(i).wait_send()
    loop(1, NZ, lambda dz: root_copy(dz).wait_send())

    loop(1, NZ, lambda dz: g_copy(0, dz).wait_recv())
    g_relay().start()

    chosen = []
    for i in NEAR:
        base = ((z + i) % NZ) * (NC * ROWS) + c * ROWS
        rows = lax.broadcasted_iota(jnp.int32, (ROWS, WIDTH), 0) + base
        hit = lax.broadcasted_iota(jnp.int32, (ROWS, WIDTH), 1) == rows
        chosen.append(jnp.where(hit, 1.0, 0.0).astype(jnp.bfloat16))

    root_relay().wait()
    left_relay().wait()
    pair_copy().wait()
    g_relay().wait()

    many = len(NEAR) * ROWS
    block = full[...].reshape(WIDTH, WIDTH)
    right = roots[...].reshape(WIDTH, WIDTH)
    across = nt(jnp.concatenate([full[(z + i) % NZ, c] for i in NEAR] + chosen, axis=0), block)
    cols = across[many:].astype(jnp.bfloat16)
    down = nn(
        jnp.concatenate(
            [lefts[i, c] for i in range(len(NEAR))] + [lefts[i, 1 - c] for i in range(len(NEAR))] + [cols], axis=0
        ),
        block,
    )
    part = nn(down[:2 * many].astype(jnp.bfloat16), right)
    tally[0] = pair[0] + pair[1] + jnp.where(lane == MOST + z % MOST, jnp.sum(part * part), 0.0)
    loop(1, NZ, lambda i: tally_copy(i).start())
    for i in range(len(NEAR)):
        at_i = slice(i * ROWS, (i + 1) * ROWS)
        box = inbox if i == 0 else outbox
        box[i, 0] = across[at_i].astype(jnp.bfloat16)
        box[i, 1] = down[2 * many + i * ROWS:2 * many + (i + 1) * ROWS].astype(jnp.bfloat16)
        box[i, 2] = part[at_i].astype(jnp.bfloat16)
        if i > 0:
            near_copy(i).start()

    for i in range(len(NEAR)):
        if i > 0:
            near_copy(i).wait_recv()
        k = (z - NEAR[i]) % MOST
        fresh[0, k] = 0.9 * stats[0, k] + 0.1 * inbox[i, 0].astype(jnp.float32)
        fresh[1, k] = 0.9 * stats[1, k] + 0.1 * inbox[i, 1].astype(jnp.float32)

    saves[0].start()
    saves[1].start()
    loop(1, NZ, lambda i: tally_copy(i).wait())
    totals = jnp.sum(tally[...], axis=0)
    entries = float(WIDTH * WIDTH)
    for i in range(len(NEAR)):
        k = (z - NEAR[i]) % MOST
        adam_total = jnp.sum(jnp.where(lane == k, totals, 0.0), axis=1, keepdims=True)
        shaped_total = jnp.sum(jnp.where(lane == MOST + k, totals, 0.0), axis=1, keepdims=True)
        ratio = jnp.sqrt(adam_total / entries) / jnp.sqrt(shaped_total / entries + 1e-06)
        turned[k] = (inbox[i, 2].astype(jnp.float32) * ratio).astype(jnp.bfloat16)
    saves[3].start()

    loop(1, NZ, lambda dz: g_copy(0, dz).wait_send())
    for i in range(1, len(NEAR)):
        near_copy(i).wait_send()
    for save in saves:
        save.wait()


def write(*refs):
    sems = refs[-1]
    half = len(refs) // 2
    copies = [pltpu.make_async_copy(refs[i], refs[half + i], sems.at[i]) for i in range(half)]
    for one in copies:
        one.start()
    for one in copies:
        one.wait()


def on_device(grads, assignment, left_stats, right_stats, second_moment, left_root, right_root):
    owner = assignment[:, 0]
    numbers = jnp.arange(BLOCKS, dtype=jnp.int32)
    earlier = numbers[None, :] < numbers[:, None]
    same = (owner[:, None] == owner[None, :]) & earlier
    rank = jnp.sum(same.astype(jnp.int32), axis=1)
    late = rank >= XFIRST
    beside = (owner[:, None] % NY == owner[None, :] % NY) & late[None, :] & earlier
    place = jnp.sum(beside.astype(jnp.int32), axis=1)

    def lookup(key, value, size, empty):
        match = key[:, None] == jnp.arange(size, dtype=jnp.int32)[None, :]
        return empty + jnp.sum(jnp.where(match, value[:, None] - empty, 0), axis=0)

    owners = NX * NY
    table = jnp.concatenate([
        lookup(jnp.where(late, -1, owner * XFIRST + rank), numbers, owners * XFIRST, BLOCKS),
        lookup(jnp.where(late, owner % NY * CROWD + place, -1), numbers, NY * CROWD, BLOCKS),
        lookup(jnp.where(late, owner * REST + rank - XFIRST, -1), place, owners * REST, CROWD),
    ])
    lean = CROWD // 2
    fits = jnp.max(jnp.where(late, place, 0)) < lean
    operands = (table, grads[0], left_stats, right_stats, second_moment, left_root, right_root)
    return lax.cond(
        fits,
        lambda *given: step(lean, 0, *given),
        lambda *given: step(CROWD, 1, *given),
        *operands,
    )


def step(cap, number, *operands):
    wide = jax.ShapeDtypeStruct((MOST, ROWS, WIDTH), jnp.float32)
    narrow = jnp.bfloat16
    dma = pltpu.SemaphoreType.DMA
    tile = (ROWS, WIDTH)
    near = len(NEAR)

    def pair(*shape):
        return [dma(shape), dma(shape)]

    outs = [wide, wide, wide, jax.ShapeDtypeStruct((MOST, ROWS, WIDTH), narrow)]
    results = pl.pallas_call(
        functools.partial(kernel, cap),
        name="shampoo",
        out_shape=outs,
        in_specs=[pl.BlockSpec(memory_space=pltpu.SMEM)] + [pl.BlockSpec(memory_space=pl.ANY)] * 6,
        out_specs=[pl.BlockSpec(memory_space=pl.ANY)] * 4,
        scratch_shapes=[
            pltpu.VMEM((3, MOST, *tile), jnp.float32),
            pltpu.VMEM((MOST, *tile), narrow),
            pltpu.VMEM((BLOCKS + 1, *tile), narrow),
            pltpu.VMEM((3, MOST, *tile), jnp.float32),
            pltpu.VMEM((2, MOST, *tile), narrow),
            pltpu.VMEM((XFIRST, NX, NY, *tile), narrow),
            pltpu.VMEM((XFIRST, NX - 1, NY, *tile), narrow),
            pltpu.VMEM((XFIRST, NY, *tile), narrow),
            pltpu.VMEM((XFIRST, NY - 1, *tile), narrow),
            pltpu.VMEM((NY, cap, *tile), narrow),
            pltpu.VMEM((NY - 1, cap, *tile), narrow),
            pltpu.VMEM((CROWD + 1, *tile), narrow),
            pltpu.VMEM((NX, REST, *tile), narrow),
            pltpu.VMEM((NX - 1, REST, *tile), narrow),
            pltpu.VMEM((MOST, *tile), narrow),
            pltpu.VMEM((NZ, NC, *tile), narrow),
            pltpu.VMEM((NZ, NC, *tile), narrow),
            pltpu.VMEM((near, NC, *tile), narrow),
            pltpu.VMEM((near, 3, *tile), narrow),
            pltpu.VMEM((near, 3, *tile), narrow),
            pltpu.VMEM((NC, 1, 128), jnp.float32),
            pltpu.VMEM((NZ, 1, 128), jnp.float32),
            dma((6,)),
            dma((4,)),
            *pair(XFIRST, NX - 1),
            *pair(XFIRST, NY - 1),
            *pair(NY - 1),
            *pair(NX - 1),
            *pair(NZ),
            *pair(1),
            *pair(NZ),
            *pair(1),
            *pair(near - 1),
            *pair(near - 1),
            *pair(1),
            *pair(NZ),
        ],
        compiler_params=pltpu.CompilerParams(
            collective_id=number, has_side_effects=True, vmem_limit_bytes=56 << 20
        ),
        cost_estimate=pl.CostEstimate(flops=800_000_000, bytes_accessed=2_400_000, transcendentals=70_000),
    )(*operands)
    return pl.pallas_call(
        write,
        name="write",
        out_shape=outs,
        in_specs=[pl.BlockSpec(memory_space=pltpu.VMEM)] * 4,
        out_specs=[pl.BlockSpec(memory_space=pl.ANY)] * 4,
        scratch_shapes=[dma((4,))],
    )(*results)


def solution(mesh):
    rows = P("dp", "replica", None)
    return jax.shard_map(
        on_device,
        mesh=mesh,
        in_specs=(P("dp", None, "replica", None), P(), rows, rows, rows, rows, rows),
        out_specs=(rows,) * 4,
        check_vma=False,
    )
```

time: 80.5 us -> 74.5 us (0.925)
  local copies, waits for them, and re-layouts: 4.7 us -> 0.65 us
  Pallas kernels: 74.1 us -> 71 us
    unnamed x12 -> x2, local copies, waits for them, and re-layouts: 4.7 us -> 0.65 us
    pallas_call x1 -> x2, Pallas kernels: 74.1 us -> 71 us  [the longest x1 69.2 us: step(): pl.pallas_call(functools.partial(kernel, cap), name='shampoo', out_shape=...]
where the time goes in v3:
time: 74.5 us; the launch traced here: 74.3 us
  Pallas kernels  71 us (95%)
  between operations  1.35 us (2%)
  other arithmetic  1.24 us (2%)
    pallas_call x1, Pallas kernels, step(): pl.pallas_call(functools.partial(kernel, cap), name='shampoo', out_shape=...  69.2 us
    pallas_call x1, Pallas kernels, step(): pl.pallas_call(write, name='write', out_shape=outs, in_specs=[pl.BlockSpe...  1.83 us

profile of v3, /device:TPU:1, one launch (start us, length us, event | category | flops | bytes accessed | tf_op | source)
XLA Modules:
  0.0 74.3 jit_solution(8189370245633421412)
XLA Ops:
  0.6 0.0 copy-start
  0.6 0.6 copy-done
  1.3 0.2 convert_reduce_fusion.1
  1.5 0.2 convert_reduce_fusion
  1.7 0.6 broadcast_add_fusion
  3.0 0.1 select_reduce_fusion.2
  3.2 0.1 pad_add_fusion
  3.2 71.0 %conditional.1 = ((f32[4,16,512]{2,1,0:T(8,128)}, f32[4,16,512]{2,1,0:T(8,128)}, f32[4,16,512]{2,1,0:T(8,128)}, bf16[4,16,512]{2,1,0:T(8,128)(2,1)})) conditional(s32[]{:T(128)} %convert_element_type.11, (s32[192]{0:T(256)S(1)}, bf16[1,64,16,512]{3,2,1,0:T(8,128)(2,1)}, f32[4,16,512]{2,1,0:T(8,128)}, f32[4,16,512]{2,1,0:T(8,128)}, ...), branch_computations={%region_6.7_spmd, %region_7.8_spmd} | conditional | flops 800000000 | bytes 2400008 | solution.py:377
  3.2 69.2 %shampoo.3 = (f32[4,16,512]{2,1,0:T(8,128)}, f32[4,16,512]{2,1,0:T(8,128)}, f32[4,16,512]{2,1,0:T(8,128)}, bf16[4,16,512]{2,1,0:T(8,128)(2,1)}) custom-call(s32[192]{0:T(256)S(1)} %get-tuple-element.39.table, bf16[64,16,512]{2,1,0:T(8,128)(2,1)} %bitcast.33, f32[4,16,512]{2,1,0:T(8,128)} %get-tuple-element.81.left_stats, ...), custom_call_target="tpu_custom_call" | custom-call | flops 800000000 | bytes 2400000 | tf_op jit(solution)/shard_map/cond/branch_1_fun/shampoo/pallas_call | solution.py:396
  72.4 1.8 %write.3 = (f32[4,16,512]{2,1,0:T(8,128)}, f32[4,16,512]{2,1,0:T(8,128)}, f32[4,16,512]{2,1,0:T(8,128)}, bf16[4,16,512]{2,1,0:T(8,128)(2,1)}) custom-call(f32[4,16,512]{2,1,0:T(8,128)} %get-tuple-element.46.refs_0_, f32[4,16,512]{2,1,0:T(8,128)} %get-tuple-element.47.refs_1_, f32[4,16,512]{2,1,0:T(8,128)} %get-tuple-element.48.refs_2_, ...), custom_call_target="tpu_custom_call" | custom-call | tf_op jit(solution)/shard_map/cond/branch_1_fun/write/pallas_call | solution.py:445
  (8 shorter events, 0.1 us)
Async XLA Ops:
  0.6 0.7 copy-start

commit v4 on v3

--- a/solution.py
+++ b/solution.py
@@ -10,9 +10,9 @@
 MESH = pl.DeviceIdType.MESH
 NX, NY, NZ, NC = 4, 8, 16, 2
 MOST, ROWS, WIDTH, BLOCKS = 4, 16, 512, 64
-XFIRST = 2
-REST = MOST - XFIRST
-CROWD = REST * NX
+FULL = 2
+REST = MOST - FULL
+CROWD = REST * NY
 NEAR = (0, -1, 1, 2)
 
 
@@ -29,7 +29,7 @@
     left_new, right_new, moment_new, direction,
     fresh, turned, blocks, stats, mine, sendx, recvx, sendy, recvy, sendq, recvq, crowd, sendr, recvr,
     low, full, roots, lefts, outbox, inbox, pair, tally,
-    load_sem, save_sem, xs, xr, ys, yr, qs, qr, ps, pr, rs, rr, us, ur, gs, gr, cs, cr, ns, nr, ls, lr, vs, vr, ts, tr,
+    load_sem, save_sem, hello, xs, xr, ys, yr, qs, qr, ps, pr, rs, rr, us, ur, gs, gr, cs, cr, ns, nr, ls, lr, vs, vr, ts, tr,
 ):
     d, r = lax.axis_index("dp"), lax.axis_index("replica")
     x, y, z, c = d // NY, d % NY, r // NC, r % NC
@@ -78,19 +78,23 @@
         pl.semaphore_signal(barrier, inc=1, device_id=at(dx=i), device_id_type=MESH)
     for i in range(1, NY):
         pl.semaphore_signal(barrier, inc=1, device_id=at(dy=i), device_id_type=MESH)
-    loop(1, NZ, lambda i: pl.semaphore_signal(
-        barrier, inc=1, device_id=at(dz=i), device_id_type=MESH
-    ))
+    for i in (-2, -1, 1, 2):
+        pl.semaphore_signal(barrier, inc=1, device_id=at(dz=i), device_id_type=MESH)
     pl.semaphore_signal(barrier, inc=1, device_id=at(dc=1), device_id_type=MESH)
 
     blocks[BLOCKS] = jnp.zeros((ROWS, WIDTH), jnp.bfloat16)
     crowd[CROWD] = jnp.zeros((ROWS, WIDTH), jnp.bfloat16)
+
+
+    def greet(number, far):
+        for i in (-far, far):
+            pl.semaphore_signal(hello.at[number], inc=1, device_id=at(dz=i), device_id_type=MESH)
 
 
     def pick(k):
         def one(i):
             to, row = i // NY, i % NY
-            sendx[k, to, row] = blocks[table[(((x + to) % NX) * NY + row) * XFIRST + k]]
+            sendx[k, to, row] = blocks[table[(((x + to) % NX) * NY + row) * FULL + k]]
 
         loop(0, NX * NY, one)
 
@@ -131,23 +135,23 @@
         low[k] = total.astype(jnp.bfloat16)
 
 
-    def pick_last():
+    def pick_rest():
         def one(i):
             to, row = i // cap, i % cap
-            sendq[to, row] = blocks[table[BLOCKS + ((y + to) % NY) * CROWD + row]]
-
-        loop(0, NY * cap, one)
+            sendq[to, row] = blocks[table[BLOCKS + ((x + to) % NX) * CROWD + row]]
+
+        loop(0, NX * cap, one)
 
     def q_copy(i):
-        return copy(sendq.at[i], recvq.at[i - 1], qs.at[i - 1], qr.at[i - 1], at(dy=i))
+        return copy(sendq.at[i], recvq.at[i - 1], qs.at[i - 1], qr.at[i - 1], at(dx=i))
 
     def q_sum():
-        for i in range(1, NY):
+        for i in range(1, NX):
             q_copy(i).wait_recv()
 
         def one(row):
             total = sendq[0, row].astype(jnp.float32)
-            for i in range(NY - 1):
+            for i in range(NX - 1):
                 total += recvq[i, row].astype(jnp.float32)
             crowd[row] = total.astype(jnp.bfloat16)
 
@@ -155,20 +159,20 @@
 
         def spread(i):
             to, row = i // REST, i % REST
-            sendr[to, row] = crowd[table[2 * BLOCKS + (to * NY + y) * REST + row]]
-
-        loop(0, NX * REST, spread)
+            sendr[to, row] = crowd[table[BLOCKS + NX * CROWD + (x * NY + to) * REST + row]]
+
+        loop(0, NY * REST, spread)
 
     def p_copy(i):
-        return copy(sendr.at[(x + i) % NX], recvr.at[i - 1], ps.at[i - 1], pr.at[i - 1], at(dx=i))
+        return copy(sendr.at[(y + i) % NY], recvr.at[i - 1], ps.at[i - 1], pr.at[i - 1], at(dy=i))
 
     def p_sum():
-        for i in range(1, NX):
+        for i in range(1, NY):
             p_copy(i).wait_recv()
-        total = sendr[x].astype(jnp.float32)
-        for i in range(NX - 1):
+        total = sendr[y].astype(jnp.float32)
+        for i in range(NY - 1):
             total += recvr[i].astype(jnp.float32)
-        low[pl.ds(XFIRST, REST)] = total.astype(jnp.bfloat16)
+        low[pl.ds(FULL, REST)] = total.astype(jnp.bfloat16)
 
 
     def root_copy(dz):
@@ -204,8 +208,8 @@
     def pair_copy():
         return copy(pair.at[0], pair.at[1], ts.at[0], tr.at[0], at(dc=1))
 
-    def near_copy(i):
-        return copy(outbox.at[i], inbox.at[i], ns.at[i - 1], nr.at[i - 1], at(dz=NEAR[i]))
+    def near_copy(part, i):
+        return copy(outbox.at[i, part], inbox.at[i, part], ns.at[part, i - 1], nr.at[part, i - 1], at(dz=NEAR[i]))
 
     def left_copy(i):
         return copy(
@@ -217,40 +221,48 @@
         return copy(piece, piece, vs.at[0], vr.at[0], at(dc=1))
 
     loads[0].wait()
+    pick_rest()
     pick(0)
-    pick_last()
-    pl.semaphore_wait(barrier, NX - 1 + NY - 1 + NZ - 1 + NC - 1)
+    pl.semaphore_wait(barrier, NX - 1 + NY - 1 + 4 + NC - 1)
+    greet(0, 2)
+    for i in range(1, NX):
+        q_copy(i).start()
     x_send(0)
-    for i in range(1, NY):
-        q_copy(i).start()
     pick(1)
-    x_send(1)
     loads[1].wait()
     loads[2].wait()
-    loop(1, NZ, lambda dz: root_copy(dz).start())
-    roots[z, c] = mine[1, z % MOST]
     lefts[0, c] = mine[0, z % MOST]
     for i in range(1, len(NEAR)):
         left_copy(i).start()
+    roots[z, c] = mine[1, z % MOST]
+    for dz in (1, 2, 14, 15):
+        root_copy(dz).start()
+    pl.semaphore_wait(hello.at[0], 2)
+    greet(1, 4)
+    for dz in (3, 4, 12, 13):
+        root_copy(dz).start()
+    q_sum()
+    x_send(1)
+    for i in range(1, NY):
+        p_copy(i).start()
+    pl.semaphore_wait(hello.at[1], 2)
+    loop(5, 12, lambda dz: root_copy(dz).start())
     x_sum(0)
     y_send(0)
+    for i in range(1, len(NEAR)):
+        left_copy(i).wait()
+    left_relay().start()
+    p_sum()
+    g_send(2)
+    g_send(3)
     x_sum(1)
     y_send(1)
     y_sum(0)
     g_send(0)
-    q_sum()
-    for i in range(1, NX):
-        p_copy(i).start()
-    for i in range(1, len(NEAR)):
-        left_copy(i).wait()
-    left_relay().start()
+    loop(1, NZ, lambda dz: root_copy(dz).wait_recv())
+    root_relay().start()
     y_sum(1)
     g_send(1)
-    p_sum()
-    g_send(2)
-    g_send(3)
-    loop(1, NZ, lambda dz: root_copy(dz).wait_recv())
-    root_relay().start()
 
     lane = lax.broadcasted_iota(jnp.int32, (1, 128), 1)
     sums = jnp.zeros((1, 128), jnp.float32)
@@ -265,14 +277,14 @@
     saves[2].start()
     pair[0] = sums
     pair_copy().start()
-    for k in range(XFIRST):
+    for k in range(FULL):
         for i in range(1, NX):
             x_copy(k, i).wait_send()
         for i in range(1, NY):
             y_copy(k, i).wait_send()
+    for i in range(1, NX):
+        q_copy(i).wait_send()
     for i in range(1, NY):
-        q_copy(i).wait_send()
-    for i in range(1, NX):
         p_copy(i).wait_send()
     loop(1, NZ, lambda dz: root_copy(dz).wait_send())
 
@@ -296,6 +308,15 @@
     right = roots[...].reshape(WIDTH, WIDTH)
     across = nt(jnp.concatenate([full[(z + i) % NZ, c] for i in NEAR] + chosen, axis=0), block)
     cols = across[many:].astype(jnp.bfloat16)
+
+    def deliver(part, values):
+        for i in range(len(NEAR)):
+            box = inbox if i == 0 else outbox
+            box[i, part] = values[i * ROWS:(i + 1) * ROWS].astype(jnp.bfloat16)
+            if i > 0:
+                near_copy(part, i).start()
+
+    deliver(0, across[:many])
     down = nn(
         jnp.concatenate(
             [lefts[i, c] for i in range(len(NEAR))] + [lefts[i, 1 - c] for i in range(len(NEAR))] + [cols], axis=0
@@ -305,24 +326,20 @@
     part = nn(down[:2 * many].astype(jnp.bfloat16), right)
     tally[0] = pair[0] + pair[1] + jnp.where(lane == MOST + z % MOST, jnp.sum(part * part), 0.0)
     loop(1, NZ, lambda i: tally_copy(i).start())
-    for i in range(len(NEAR)):
-        at_i = slice(i * ROWS, (i + 1) * ROWS)
-        box = inbox if i == 0 else outbox
-        box[i, 0] = across[at_i].astype(jnp.bfloat16)
-        box[i, 1] = down[2 * many + i * ROWS:2 * many + (i + 1) * ROWS].astype(jnp.bfloat16)
-        box[i, 2] = part[at_i].astype(jnp.bfloat16)
-        if i > 0:
-            near_copy(i).start()
-
-    for i in range(len(NEAR)):
-        if i > 0:
-            near_copy(i).wait_recv()
-        k = (z - NEAR[i]) % MOST
-        fresh[0, k] = 0.9 * stats[0, k] + 0.1 * inbox[i, 0].astype(jnp.float32)
-        fresh[1, k] = 0.9 * stats[1, k] + 0.1 * inbox[i, 1].astype(jnp.float32)
-
-    saves[0].start()
-    saves[1].start()
+    deliver(1, down[2 * many:])
+    deliver(2, part[:many])
+
+    for j in range(2):
+        for i in range(len(NEAR)):
+            if i > 0:
+                near_copy(j, i).wait()
+            k = (z - NEAR[i]) % MOST
+            fresh[j, k] = 0.9 * stats[j, k] + 0.1 * inbox[i, j].astype(jnp.float32)
+        saves[j].start()
+
+    for i in range(1, len(NEAR)):
+        near_copy(2, i).wait()
+    loop(1, NZ, lambda dz: g_copy(0, dz).wait_send())
     loop(1, NZ, lambda i: tally_copy(i).wait())
     totals = jnp.sum(tally[...], axis=0)
     entries = float(WIDTH * WIDTH)
@@ -333,22 +350,21 @@
         ratio = jnp.sqrt(adam_total / entries) / jnp.sqrt(shaped_total / entries + 1e-06)
         turned[k] = (inbox[i, 2].astype(jnp.float32) * ratio).astype(jnp.bfloat16)
     saves[3].start()
-
-    loop(1, NZ, lambda dz: g_copy(0, dz).wait_send())
-    for i in range(1, len(NEAR)):
-        near_copy(i).wait_send()
     for save in saves:
         save.wait()
 
 
 def write(*refs):
-    sems = refs[-1]
-    half = len(refs) // 2
-    copies = [pltpu.make_async_copy(refs[i], refs[half + i], sems.at[i]) for i in range(half)]
-    for one in copies:
-        one.start()
-    for one in copies:
-        one.wait()
+    sources, targets, held, into, out = refs[:4], refs[4:8], refs[8:12], refs[12], refs[13]
+    loads = [pltpu.make_async_copy(sources[i], held[i], into.at[i]) for i in range(4)]
+    saves = [pltpu.make_async_copy(held[i], targets[i], out.at[i]) for i in range(4)]
+    for load in loads:
+        load.start()
+    for load, save in zip(loads, saves):
+        load.wait()
+        save.start()
+    for save in saves:
+        save.wait()
 
 
 def on_device(grads, assignment, left_stats, right_stats, second_moment, left_root, right_root):
@@ -357,8 +373,8 @@
     earlier = numbers[None, :] < numbers[:, None]
     same = (owner[:, None] == owner[None, :]) & earlier
     rank = jnp.sum(same.astype(jnp.int32), axis=1)
-    late = rank >= XFIRST
-    beside = (owner[:, None] % NY == owner[None, :] % NY) & late[None, :] & earlier
+    late = rank >= FULL
+    beside = (owner[:, None] // NY == owner[None, :] // NY) & late[None, :] & earlier
     place = jnp.sum(beside.astype(jnp.int32), axis=1)
 
     def lookup(key, value, size, empty):
@@ -367,11 +383,11 @@
 
     owners = NX * NY
     table = jnp.concatenate([
-        lookup(jnp.where(late, -1, owner * XFIRST + rank), numbers, owners * XFIRST, BLOCKS),
-        lookup(jnp.where(late, owner % NY * CROWD + place, -1), numbers, NY * CROWD, BLOCKS),
-        lookup(jnp.where(late, owner * REST + rank - XFIRST, -1), place, owners * REST, CROWD),
+        lookup(jnp.where(late, -1, owner * FULL + rank), numbers, owners * FULL, BLOCKS),
+        lookup(jnp.where(late, owner // NY * CROWD + place, -1), numbers, NX * CROWD, BLOCKS),
+        lookup(jnp.where(late, owner * REST + rank - FULL, -1), place, owners * REST, CROWD),
     ])
-    lean = CROWD // 2
+    lean = CROWD * 3 // 8
     fits = jnp.max(jnp.where(late, place, 0)) < lean
     operands = (table, grads[0], left_stats, right_stats, second_moment, left_root, right_root)
     return lax.cond(
@@ -405,15 +421,15 @@
             pltpu.VMEM((BLOCKS + 1, *tile), narrow),
             pltpu.VMEM((3, MOST, *tile), jnp.float32),
             pltpu.VMEM((2, MOST, *tile), narrow),
-            pltpu.VMEM((XFIRST, NX, NY, *tile), narrow),
-            pltpu.VMEM((XFIRST, NX - 1, NY, *tile), narrow),
-            pltpu.VMEM((XFIRST, NY, *tile), narrow),
-            pltpu.VMEM((XFIRST, NY - 1, *tile), narrow),
-            pltpu.VMEM((NY, cap, *tile), narrow),
-            pltpu.VMEM((NY - 1, cap, *tile), narrow),
+            pltpu.VMEM((FULL, NX, NY, *tile), narrow),
+            pltpu.VMEM((FULL, NX - 1, NY, *tile), narrow),
+            pltpu.VMEM((FULL, NY, *tile), narrow),
+            pltpu.VMEM((FULL, NY - 1, *tile), narrow),
+            pltpu.VMEM((NX, cap, *tile), narrow),
+            pltpu.VMEM((NX - 1, cap, *tile), narrow),
             pltpu.VMEM((CROWD + 1, *tile), narrow),
-            pltpu.VMEM((NX, REST, *tile), narrow),
-            pltpu.VMEM((NX - 1, REST, *tile), narrow),
+            pltpu.VMEM((NY, REST, *tile), narrow),
+            pltpu.VMEM((NY - 1, REST, *tile), narrow),
             pltpu.VMEM((MOST, *tile), narrow),
             pltpu.VMEM((NZ, NC, *tile), narrow),
             pltpu.VMEM((NZ, NC, *tile), narrow),
@@ -424,15 +440,16 @@
             pltpu.VMEM((NZ, 1, 128), jnp.float32),
             dma((6,)),
             dma((4,)),
-            *pair(XFIRST, NX - 1),
-            *pair(XFIRST, NY - 1),
+            pltpu.SemaphoreType.REGULAR((2,)),
+            *pair(FULL, NX - 1),
+            *pair(FULL, NY - 1),
+            *pair(NX - 1),
             *pair(NY - 1),
-            *pair(NX - 1),
             *pair(NZ),
             *pair(1),
             *pair(NZ),
             *pair(1),
-            *pair(near - 1),
+            *pair(3, near - 1),
             *pair(near - 1),
             *pair(1),
             *pair(NZ),
@@ -446,9 +463,10 @@
         write,
         name="write",
         out_shape=outs,
-        in_specs=[pl.BlockSpec(memory_space=pltpu.VMEM)] * 4,
+        in_specs=[pl.BlockSpec(memory_space=pl.ANY)] * 4,
         out_specs=[pl.BlockSpec(memory_space=pl.ANY)] * 4,
-        scratch_shapes=[dma((4,))],
+        scratch_shapes=[pltpu.VMEM(one.shape, one.dtype) for one in outs] + pair(4),
+        compiler_params=pltpu.CompilerParams(vmem_limit_bytes=56 << 20),
     )(*results)
 
 

time: 74.5 us -> 70.2 us (0.942)
  Pallas kernels: 71 us -> 66.7 us
    pallas_call x1, Pallas kernels: 69.2 us -> 64.9 us  [step(): pl.pallas_call(functools.partial(kernel, cap), name='shampoo', out_shape=...]
where the time goes in v4:
time: 70.2 us; the launch traced here: 69.9 us
  Pallas kernels  66.7 us (95%)
  between operations  1.35 us (2%)
  other arithmetic  1.24 us (2%)
    pallas_call x1, Pallas kernels, step(): pl.pallas_call(functools.partial(kernel, cap), name='shampoo', out_shape=...  64.9 us
    pallas_call x1, Pallas kernels, step(): pl.pallas_call(write, name='write', out_shape=outs, in_specs=[pl.BlockSpe...  1.77 us

profile of v4, /device:TPU:1, one launch (start us, length us, event | category | flops | bytes accessed | tf_op | source)
XLA Modules:
  0.0 69.9 jit_solution(13069863622237647879)
XLA Ops:
  0.6 0.0 copy-start
  0.6 0.6 copy-done
  1.3 0.2 convert_reduce_fusion.1
  1.5 0.2 convert_reduce_fusion
  1.7 0.6 broadcast_add_fusion.1
  3.0 0.1 select_reduce_fusion.2
  3.2 0.1 pad_add_fusion
  3.2 66.7 %conditional.1 = ((f32[4,16,512]{2,1,0:T(8,128)}, f32[4,16,512]{2,1,0:T(8,128)}, f32[4,16,512]{2,1,0:T(8,128)}, bf16[4,16,512]{2,1,0:T(8,128)(2,1)})) conditional(s32[]{:T(128)} %convert_element_type.11, (s32[192]{0:T(256)S(1)}, bf16[1,64,16,512]{3,2,1,0:T(8,128)(2,1)}, f32[4,16,512]{2,1,0:T(8,128)}, f32[4,16,512]{2,1,0:T(8,128)}, ...), branch_computations={%region_6.7_spmd, %region_7.8_spmd} | conditional | flops 800000000 | bytes 2400008 | solution.py:393
  3.2 64.9 %shampoo.3 = (f32[4,16,512]{2,1,0:T(8,128)}, f32[4,16,512]{2,1,0:T(8,128)}, f32[4,16,512]{2,1,0:T(8,128)}, bf16[4,16,512]{2,1,0:T(8,128)(2,1)}) custom-call(s32[192]{0:T(256)S(1)} %get-tuple-element.39.table, bf16[64,16,512]{2,1,0:T(8,128)(2,1)} %bitcast.33, f32[4,16,512]{2,1,0:T(8,128)} %get-tuple-element.81.left_stats, ...), custom_call_target="tpu_custom_call" | custom-call | flops 800000000 | bytes 2400000 | tf_op jit(solution)/shard_map/cond/branch_1_fun/shampoo/pallas_call | solution.py:412
  68.2 1.8 %write.3 = (f32[4,16,512]{2,1,0:T(8,128)}, f32[4,16,512]{2,1,0:T(8,128)}, f32[4,16,512]{2,1,0:T(8,128)}, bf16[4,16,512]{2,1,0:T(8,128)(2,1)}) custom-call(f32[4,16,512]{2,1,0:T(8,128)} %get-tuple-element.46.refs_0_, f32[4,16,512]{2,1,0:T(8,128)} %get-tuple-element.47.refs_1_, f32[4,16,512]{2,1,0:T(8,128)} %get-tuple-element.48.refs_2_, ...), custom_call_target="tpu_custom_call" | custom-call | tf_op jit(solution)/shard_map/cond/branch_1_fun/write/pallas_call | solution.py:462
  (8 shorter events, 0.1 us)
Async XLA Ops:
  0.6 0.7 copy-start

commit v5 on v4

--- a/solution.py
+++ b/solution.py
@@ -48,6 +48,12 @@
             return carry
 
         lax.fori_loop(start, stop, step, 0)
+
+    barrier = pltpu.get_barrier_semaphore()
+    nearby = [at(dx=i) for i in (1, 2, 3)] + [at(dc=1)]
+    nearby += [at(dy=i) for i in (-2, -1, 1, 2)] + [at(dz=i) for i in (-2, -1, 1, 2)]
+    for device in nearby:
+        pl.semaphore_signal(barrier, inc=1, device_id=device, device_id_type=MESH)
 
     loads = [
         pltpu.make_async_copy(a, b, load_sem.at[i])
@@ -73,22 +79,13 @@
         ))
     ]
 
-    barrier = pltpu.get_barrier_semaphore()
-    for i in range(1, NX):
-        pl.semaphore_signal(barrier, inc=1, device_id=at(dx=i), device_id_type=MESH)
-    for i in range(1, NY):
-        pl.semaphore_signal(barrier, inc=1, device_id=at(dy=i), device_id_type=MESH)
-    for i in (-2, -1, 1, 2):
-        pl.semaphore_signal(barrier, inc=1, device_id=at(dz=i), device_id_type=MESH)
-    pl.semaphore_signal(barrier, inc=1, device_id=at(dc=1), device_id_type=MESH)
-
     blocks[BLOCKS] = jnp.zeros((ROWS, WIDTH), jnp.bfloat16)
     crowd[CROWD] = jnp.zeros((ROWS, WIDTH), jnp.bfloat16)
 
 
-    def greet(number, far):
-        for i in (-far, far):
-            pl.semaphore_signal(hello.at[number], inc=1, device_id=at(dz=i), device_id_type=MESH)
+    def greet(number, *devices):
+        for device in devices:
+            pl.semaphore_signal(hello.at[number], inc=1, device_id=device, device_id_type=MESH)
 
 
     def pick(k):
@@ -222,11 +219,11 @@
 
     loads[0].wait()
     pick_rest()
-    pick(0)
-    pl.semaphore_wait(barrier, NX - 1 + NY - 1 + 4 + NC - 1)
-    greet(0, 2)
+    pl.semaphore_wait(barrier, len(nearby))
+    greet(0, at(dy=-2), at(dy=2), at(dz=-2), at(dz=2))
     for i in range(1, NX):
         q_copy(i).start()
+    pick(0)
     x_send(0)
     pick(1)
     loads[1].wait()
@@ -237,8 +234,8 @@
     roots[z, c] = mine[1, z % MOST]
     for dz in (1, 2, 14, 15):
         root_copy(dz).start()
-    pl.semaphore_wait(hello.at[0], 2)
-    greet(1, 4)
+    pl.semaphore_wait(hello.at[0], 4)
+    greet(1, at(dz=-4), at(dz=4))
     for dz in (3, 4, 12, 13):
         root_copy(dz).start()
     q_sum()
@@ -306,8 +303,6 @@
     many = len(NEAR) * ROWS
     block = full[...].reshape(WIDTH, WIDTH)
     right = roots[...].reshape(WIDTH, WIDTH)
-    across = nt(jnp.concatenate([full[(z + i) % NZ, c] for i in NEAR] + chosen, axis=0), block)
-    cols = across[many:].astype(jnp.bfloat16)
 
     def deliver(part, values):
         for i in range(len(NEAR)):
@@ -316,18 +311,15 @@
             if i > 0:
                 near_copy(part, i).start()
 
-    deliver(0, across[:many])
-    down = nn(
-        jnp.concatenate(
-            [lefts[i, c] for i in range(len(NEAR))] + [lefts[i, 1 - c] for i in range(len(NEAR))] + [cols], axis=0
-        ),
-        block,
-    )
-    part = nn(down[:2 * many].astype(jnp.bfloat16), right)
+    lanes = [lefts[i, c] for i in range(len(NEAR))] + [lefts[i, 1 - c] for i in range(len(NEAR))]
+    product = nn(jnp.concatenate(lanes, axis=0), block).astype(jnp.bfloat16)
+    part = nn(product, right)
     tally[0] = pair[0] + pair[1] + jnp.where(lane == MOST + z % MOST, jnp.sum(part * part), 0.0)
     loop(1, NZ, lambda i: tally_copy(i).start())
-    deliver(1, down[2 * many:])
     deliver(2, part[:many])
+    across = nt(jnp.concatenate([full[(z + i) % NZ, c] for i in NEAR] + chosen, axis=0), block)
+    deliver(0, across[:many])
+    deliver(1, nn(across[many:].astype(jnp.bfloat16), block))
 
     for j in range(2):
         for i in range(len(NEAR)):

time: 70.2 us -> 69.7 us (level)
  no operation moved by 1% of the time
where the time goes in v5:
time: 69.7 us; the launch traced here: 69.5 us
  Pallas kernels  66.3 us (95%)
  between operations  1.35 us (2%)
  other arithmetic  1.24 us (2%)
    pallas_call x1, Pallas kernels, step(): pl.pallas_call(functools.partial(kernel, cap), name='shampoo', out_shape=...  64.5 us
    pallas_call x1, Pallas kernels, step(): pl.pallas_call(write, name='write', out_shape=outs, in_specs=[pl.BlockSpe...  1.77 us

profile of v5, /device:TPU:1, one launch (start us, length us, event | category | flops | bytes accessed | tf_op | source)
XLA Modules:
  0.0 69.5 jit_solution(16285509526379113881)
XLA Ops:
  0.6 0.0 copy-start
  0.6 0.6 copy-done
  1.3 0.2 convert_reduce_fusion.1
  1.5 0.2 convert_reduce_fusion
  1.7 0.6 broadcast_add_fusion.1
  3.0 0.1 select_reduce_fusion.2
  3.2 0.1 pad_add_fusion
  3.2 66.3 %conditional.1 = ((f32[4,16,512]{2,1,0:T(8,128)}, f32[4,16,512]{2,1,0:T(8,128)}, f32[4,16,512]{2,1,0:T(8,128)}, bf16[4,16,512]{2,1,0:T(8,128)(2,1)})) conditional(s32[]{:T(128)} %convert_element_type.11, (s32[192]{0:T(256)S(1)}, bf16[1,64,16,512]{3,2,1,0:T(8,128)(2,1)}, f32[4,16,512]{2,1,0:T(8,128)}, f32[4,16,512]{2,1,0:T(8,128)}, ...), branch_computations={%region_6.7_spmd, %region_7.8_spmd} | conditional | flops 800000000 | bytes 2400008 | solution.py:385
  3.2 64.5 %shampoo.3 = (f32[4,16,512]{2,1,0:T(8,128)}, f32[4,16,512]{2,1,0:T(8,128)}, f32[4,16,512]{2,1,0:T(8,128)}, bf16[4,16,512]{2,1,0:T(8,128)(2,1)}) custom-call(s32[192]{0:T(256)S(1)} %get-tuple-element.39.table, bf16[64,16,512]{2,1,0:T(8,128)(2,1)} %bitcast.33, f32[4,16,512]{2,1,0:T(8,128)} %get-tuple-element.81.left_stats, ...), custom_call_target="tpu_custom_call" | custom-call | flops 800000000 | bytes 2400000 | tf_op jit(solution)/shard_map/cond/branch_1_fun/shampoo/pallas_call | solution.py:404
  67.8 1.8 %write.3 = (f32[4,16,512]{2,1,0:T(8,128)}, f32[4,16,512]{2,1,0:T(8,128)}, f32[4,16,512]{2,1,0:T(8,128)}, bf16[4,16,512]{2,1,0:T(8,128)(2,1)}) custom-call(f32[4,16,512]{2,1,0:T(8,128)} %get-tuple-element.46.refs_0_, f32[4,16,512]{2,1,0:T(8,128)} %get-tuple-element.47.refs_1_, f32[4,16,512]{2,1,0:T(8,128)} %get-tuple-element.48.refs_2_, ...), custom_call_target="tpu_custom_call" | custom-call | tf_op jit(solution)/shard_map/cond/branch_1_fun/write/pallas_call | solution.py:454
  (8 shorter events, 0.1 us)
Async XLA Ops:
  0.6 0.7 copy-start

commit v6 on v5

--- a/solution.py
+++ b/solution.py
@@ -66,8 +66,7 @@
             (right_stats, stats.at[1]),
         ))
     ]
-    for load in loads:
-        load.start()
+    loads[0].start()
 
     saves = [
         pltpu.make_async_copy(a, b, save_sem.at[i])
@@ -223,6 +222,8 @@
     greet(0, at(dy=-2), at(dy=2), at(dz=-2), at(dz=2))
     for i in range(1, NX):
         q_copy(i).start()
+    for load in loads[1:]:
+        load.start()
     pick(0)
     x_send(0)
     pick(1)

time: 69.7 us -> 69.7 us (level)
  no operation moved by 1% of the time
where the time goes in v6:
time: 69.7 us; the launch traced here: 69.5 us
  Pallas kernels  66.3 us (95%)
  between operations  1.35 us (2%)
  other arithmetic  1.24 us (2%)
    pallas_call x1, Pallas kernels, step(): pl.pallas_call(functools.partial(kernel, cap), name='shampoo', out_shape=...  64.5 us
    pallas_call x1, Pallas kernels, step(): pl.pallas_call(write, name='write', out_shape=outs, in_specs=[pl.BlockSpe...  1.77 us

profile of v6, /device:TPU:1, one launch (start us, length us, event | category | flops | bytes accessed | tf_op | source)
XLA Modules:
  0.0 69.5 jit_solution(15761784202020588742)
XLA Ops:
  0.6 0.0 copy-start
  0.6 0.6 copy-done
  1.3 0.2 convert_reduce_fusion.1
  1.5 0.2 convert_reduce_fusion
  1.7 0.6 broadcast_add_fusion.1
  3.0 0.1 select_reduce_fusion.2
  3.2 0.1 pad_add_fusion
  3.2 66.3 %conditional.1 = ((f32[4,16,512]{2,1,0:T(8,128)}, f32[4,16,512]{2,1,0:T(8,128)}, f32[4,16,512]{2,1,0:T(8,128)}, bf16[4,16,512]{2,1,0:T(8,128)(2,1)})) conditional(s32[]{:T(128)} %convert_element_type.11, (s32[192]{0:T(256)S(1)}, bf16[1,64,16,512]{3,2,1,0:T(8,128)(2,1)}, f32[4,16,512]{2,1,0:T(8,128)}, f32[4,16,512]{2,1,0:T(8,128)}, ...), branch_computations={%region_6.7_spmd, %region_7.8_spmd} | conditional | flops 800000000 | bytes 2400008 | solution.py:386
  3.2 64.5 %shampoo.3 = (f32[4,16,512]{2,1,0:T(8,128)}, f32[4,16,512]{2,1,0:T(8,128)}, f32[4,16,512]{2,1,0:T(8,128)}, bf16[4,16,512]{2,1,0:T(8,128)(2,1)}) custom-call(s32[192]{0:T(256)S(1)} %get-tuple-element.39.table, bf16[64,16,512]{2,1,0:T(8,128)(2,1)} %bitcast.33, f32[4,16,512]{2,1,0:T(8,128)} %get-tuple-element.81.left_stats, ...), custom_call_target="tpu_custom_call" | custom-call | flops 800000000 | bytes 2400000 | tf_op jit(solution)/shard_map/cond/branch_1_fun/shampoo/pallas_call | solution.py:405
  67.8 1.8 %write.3 = (f32[4,16,512]{2,1,0:T(8,128)}, f32[4,16,512]{2,1,0:T(8,128)}, f32[4,16,512]{2,1,0:T(8,128)}, bf16[4,16,512]{2,1,0:T(8,128)(2,1)}) custom-call(f32[4,16,512]{2,1,0:T(8,128)} %get-tuple-element.46.refs_0_, f32[4,16,512]{2,1,0:T(8,128)} %get-tuple-element.47.refs_1_, f32[4,16,512]{2,1,0:T(8,128)} %get-tuple-element.48.refs_2_, ...), custom_call_target="tpu_custom_call" | custom-call | tf_op jit(solution)/shard_map/cond/branch_1_fun/write/pallas_call | solution.py:455
  (8 shorter events, 0.1 us)
Async XLA Ops:
  0.6 0.7 copy-start
